TPU v7x, 32 devices: a whole 2x2x4 slice. The times are simulated.
32 devices in a mesh: inst: 8 (over z, x), head: 4 (over y, core).
Axes of the slice: x: 2, y: 2, z: 4, core: 2. Of those that a mesh axis runs over, the one named last changes fastest.
Arguments:
- cache_keys: bfloat16 [1024, 64, 8, 128], P('inst', None, 'head'), may hold values from -10 to 10
- cache_values: bfloat16 [1024, 64, 8, 128], P('inst', None, 'head'), may hold values from -6 to 6
- slot_req: int32 [1024], P('inst'), may hold values from 0 to 11, as said below
- slot_fill: int32 [1024], P('inst'), may hold values from 0 to 64, as said below
- mig_src: int32 [8, 8, 2], P('inst'), may hold values from -1 to 127, as said below
- mig_dst: int32 [8, 8, 2], P('inst'), may hold values from -1 to 71, as said below
- queries: bfloat16 [16, 12, 128, 128], P(None, None, 'head'), may hold values from -64 to 64
- new_keys: bfloat16 [16, 12, 8, 128], P(None, None, 'head'), may hold values from -10 to 10
- new_values: bfloat16 [16, 12, 8, 128], P(None, None, 'head'), may hold values from -6 to 6
- out_weight: bfloat16 [16384, 16384], P('head', 'inst'), may hold values from -0.046875 to 0.046875
Outputs:
- moved_keys: bfloat16 [1024, 64, 8, 128], P('inst', None, 'head')
- moved_values: bfloat16 [1024, 64, 8, 128], P('inst', None, 'head')
- output: bfloat16 [16, 12, 16384], P(None, None, ('inst', 'head'))
Inputs may be any that keep to these rules, and one draw needn't show every extreme that they name: `slot_req`: request of each slot; requests hold very different numbers of pages. A slot's live tokens are its first slot_fill tokens; 0 means the slot is empty. Each non-negative entry names a non-empty slot of the sending instance (first index); no slot is named twice. mig_src is -1 exactly where mig_dst is -1. At most 2 pages go from one instance to another, and some pairs carry exactly 2. `mig_dst`: each non-negative entry names an empty slot of the receiving instance (second index) that is named by no other entry and is not itself a source.
All inputs are finite; a program needn't handle non-finite values.
Results may differ from a plain program's by a relative error of at most 0.0051.
Values may be sent and summed in bfloat16 or wider, within the bound.
No kernel may reach another device: no remote copies, remote signals or barrier semaphores. Data moves between devices by JAX's collectives and lax.ppermute only.
A program may use at most 256 MiB of HBM per device.

v0:
```python
import math

import jax
import jax.numpy as jnp
from jax import lax
from jax.sharding import PartitionSpec as P

masked_score = -1e30


def flatten_heads(values):
    step_count, requests = (values.shape[2], values.shape[0])
    return values.transpose(2, 0, 1, 3, 4).reshape(step_count, requests, -1)


def shards(
    cache_keys,
    cache_values,
    slot_req,
    slot_fill,
    mig_src,
    mig_dst,
    queries,
    new_keys,
    new_values,
    out_weight,
):
    slot_count, page_len, kv_local, head_dim = cache_keys.shape
    step_count, requests, heads_local, _ = queries.shape
    group_size = heads_local // kv_local
    score_scale = 1.0 / math.sqrt(head_dim)
    peer_count = lax.axis_size("inst")
    capacity = mig_src.shape[2]
    outgoing = mig_src[0].reshape(-1)
    landing = mig_dst[0].reshape(-1)
    leaving = outgoing >= 0
    picked = jnp.maximum(outgoing, 0)
    parcel = jnp.stack([cache_keys[picked], cache_values[picked]], axis=1)
    parcel = parcel.reshape(peer_count, capacity, 2, page_len, kv_local, head_dim)
    labels = jnp.stack([slot_req[picked], slot_fill[picked], landing], axis=1).reshape(
        peer_count, capacity, 3
    )
    arrived, arrived_labels = (
        lax.all_to_all(parcel, "inst", split_axis=0, concat_axis=0, tiled=True),
        lax.all_to_all(labels, "inst", split_axis=0, concat_axis=0, tiled=True),
    )
    arrived = arrived.reshape(peer_count * capacity, 2, page_len, kv_local, head_dim)
    arrived_labels = arrived_labels.reshape(peer_count * capacity, 3)
    vacated = jnp.where(leaving, outgoing, slot_count)
    target = jnp.where(arrived_labels[:, 2] >= 0, arrived_labels[:, 2], slot_count)
    moved_keys = (
        cache_keys.at[vacated]
        .set(jnp.zeros_like(parcel[0, 0, 0]), mode="drop")
        .at[target]
        .set(arrived[:, 0], mode="drop")
    )
    moved_values = (
        cache_values.at[vacated]
        .set(jnp.zeros_like(parcel[0, 0, 1]), mode="drop")
        .at[target]
        .set(arrived[:, 1], mode="drop")
    )
    moved_req = slot_req.at[target].set(arrived_labels[:, 0], mode="drop")
    moved_fill = (
        slot_fill.at[vacated].set(0, mode="drop").at[target].set(arrived_labels[:, 1], mode="drop")
    )
    keys, values, req_used, fill_used = (moved_keys, moved_values, moved_req, moved_fill)
    grouped = queries.reshape(step_count, requests, kv_local, group_size, head_dim)
    chosen = grouped[:, req_used]
    scores = (
        jnp.einsum("snkgd,ntkd->nksgt", chosen, keys, preferred_element_type=jnp.float32)
        * score_scale
    )
    live_tokens = jnp.arange(page_len, dtype=jnp.int32)[None, :] < fill_used[:, None]
    live_full = live_tokens[:, None, None, None, :]
    scores = jnp.where(live_full, scores, masked_score)
    page_peak = scores.max(-1)
    weights = jnp.where(live_full, jnp.exp(scores - page_peak[..., None]), 0.0)
    weight_sum = weights.sum(-1)
    per_slot = jnp.einsum(
        "nksgt,ntkd->nksgd",
        weights.astype(jnp.bfloat16),
        values,
        preferred_element_type=jnp.float32,
    )
    members = jnp.arange(requests, dtype=jnp.int32)
    onehot = req_used[:, None] == members[None, :]
    indicator = onehot.astype(jnp.float32)
    local_peak = jnp.where(onehot[:, :, None, None, None], page_peak[:, None], masked_score).max(0)
    fresh_part = (
        jnp.einsum("srkgd,urkd->rksgu", grouped, new_keys, preferred_element_type=jnp.float32)
        * score_scale
    )
    causal = jnp.arange(step_count)[None, :] <= jnp.arange(step_count)[:, None]
    fresh_part = jnp.where(causal[None, None, :, None, :], fresh_part, masked_score)
    fresh_peak = fresh_part.max(-1)
    fresh_weights = jnp.exp(fresh_part - fresh_peak[..., None])
    fresh_numerator = jnp.einsum(
        "rksgu,urkd->rksgd",
        fresh_weights.astype(jnp.bfloat16),
        new_values,
        preferred_element_type=jnp.float32,
    )
    fresh_denominator = fresh_weights.sum(-1)
    score_peak = lax.pmax(jnp.maximum(local_peak, fresh_peak), "inst")
    factor = jnp.exp(page_peak - score_peak[req_used])
    numerator = jnp.einsum(
        "nr,nksgd->rksgd", indicator, per_slot * factor[..., None], precision=lax.Precision.HIGHEST
    )
    denominator = jnp.einsum(
        "nr,nksg->rksg", indicator, weight_sum * factor, precision=lax.Precision.HIGHEST
    )
    fresh_factor = jnp.exp(fresh_peak - score_peak)
    numerator, denominator, fresh_numer, fresh_denom = (
        numerator,
        denominator,
        fresh_numerator * fresh_factor[..., None],
        fresh_denominator * fresh_factor,
    )
    share_width = heads_local * head_dim // peer_count
    numerator_share = lax.psum_scatter(
        flatten_heads(numerator), "inst", scatter_dimension=2, tiled=True
    )
    denominator_all = lax.psum(denominator, "inst")
    full_denominator = flatten_heads(
        jnp.broadcast_to((denominator_all + fresh_denom)[..., None], fresh_numer.shape)
    )
    offset_start = lax.axis_index("inst") * share_width
    fresh_share = lax.dynamic_slice_in_dim(flatten_heads(fresh_numer), offset_start, share_width, 2)
    share_part = (numerator_share + fresh_share) / lax.dynamic_slice_in_dim(
        full_denominator, offset_start, share_width, 2
    )
    attention = lax.all_gather(share_part.astype(jnp.bfloat16), "inst", axis=2, tiled=True)
    attention = attention.reshape(step_count * requests, heads_local * head_dim)
    projected = jnp.dot(attention, out_weight, preferred_element_type=jnp.float32).reshape(
        step_count, requests, -1
    )
    output = lax.psum_scatter(projected, "head", scatter_dimension=2, tiled=True).astype(
        jnp.bfloat16
    )
    return (moved_keys, moved_values, output)


def solution(mesh):
    in_specs = (
        P("inst", None, "head", None),
        P("inst", None, "head", None),
        P("inst"),
        P("inst"),
        P("inst", None, None),
        P("inst", None, None),
        P(None, None, "head", None),
        P(None, None, "head", None),
        P(None, None, "head", None),
        P("head", "inst"),
    )
    out_specs = (
        P("inst", None, "head", None),
        P("inst", None, "head", None),
        P(None, None, ("inst", "head")),
    )
    return jax.shard_map(shards, mesh=mesh, in_specs=in_specs, out_specs=out_specs, check_vma=False)
```

profile of v0, /device:TPU:0, one launch (start us, length us, event | category | flops | bytes accessed | tf_op | source)
XLA Modules:
  0.0 429.9 jit_solution(13222222816589372134)
XLA Ops:
  8.5 11.6 %copy.197 = bf16[128,64,2,128]{3,2,1,0:T(2,128)(2,1)} copy(bf16[128,64,2,128]{3,2,1,0:T(2,128)(2,1)} %param.10) | data formatting | bytes 8388608
  20.2 11.6 %copy.198 = bf16[128,64,2,128]{3,2,1,0:T(2,128)(2,1)} copy(bf16[128,64,2,128]{3,2,1,0:T(2,128)(2,1)} %param.11) | data formatting | bytes 8388608
  34.2 7.6 %all-to-all-start = ((s32[8,2,3]{2,1,0:T(2,128)}), s32[8,2,3]{2,1,0:T(2,128)S(1)}, u32[]{:S(2)}, u32[]{:S(2)}) async-start(s32[8,2,3]{2,1,0:T(2,128)} %copy.132), calls=%async_computation | async-start | bytes 16384 | tf_op jit(solution)/shard_map/all_to_all | solution.py:45
  41.8 3.8 gather_fusion.2
  45.6 3.8 gather_fusion.3
  51.8 6.0 %all-to-all-start.1 = ((bf16[8,2,2,64,2,128]{5,4,3,1,2,0:T(2,128)(2,1)}), bf16[8,2,2,64,2,128]{5,4,3,1,2,0:T(2,128)(2,1)S(1)}, u32[]{:S(2)}, u32[]{:S(2)}) async-start(bf16[8,2,2,64,2,128]{5,4,3,1,2,0:T(2,128)(2,1)} %pad_maximum_fusion), calls=%async_computation.1 | async-start | bytes 2097152 | tf_op jit(solution)/shard_map/all_to_all | solution.py:44
  58.3 4.1 scatter_fusion
  62.4 4.1 scatter_fusion.2
  67.2 5.6 %copy.135 = bf16[128,64,2,128]{3,1,2,0:T(8,128)(2,1)} copy(bf16[128,64,2,128]{3,2,1,0:T(2,128)(2,1)} %scatter_fusion) | data formatting | bytes 8388608 | tf_op jit(solution)/shard_map/scatter | solution.py:53
  72.8 3.3 copy.136
  76.1 5.4 %fusion.20 = (f32[12,2,16,16]{3,2,1,0:T(8,128)S(1)}, f32[12,2,16,16,16]{3,4,2,1,0:T(8,128)}) fusion(pred[16,16]{1,0:T(8,128)(4,1)S(1)} %iota_compare_fusion.1, bf16[16,12,2,128,1]{3,2,1,0,4:T(2,128)(2,1)S(1)} %bitcast.81, bf16[16,12,2,16,128]{4,3,2,1,0:T(8,128)(2,1)S(1)} %bitcast.72), kind=kOutput, calls=%fused_computation.37 | convolution fusion | flops 25454592 | bytes 2089216 | tf_op jit(solution)/shard_map/srkgd,urkd->rksgu/dot_general | solution.py:91
  82.4 8.3 %gather_fusion.4 = bf16[128,16,2,16,128]{4,3,2,1,0:T(8,128)(2,1)} fusion(bf16[16,12,2,16,128]{4,3,2,1,0:T(8,128)(2,1)S(1)} %bitcast.73, s32[1024]{0:T(1024)S(1)} %pad_clamp_fusion), kind=kCustom, calls=%fused_computation.4 | custom fusion | bytes 33554944 | tf_op jit(solution)/shard_map/gather | solution.py:69
  94.8 21.3 %fusion.2 = (f32[128,2,16,16]{3,2,1,0:T(8,128)S(1)}, f32[128,2,16,16,64]{4,3,2,1,0:T(8,128)}) fusion(pred[128,64]{1,0:T(8,128)(4,1)S(1)} %iota_compare_fusion, bf16[128,64,2,128]{3,1,2,0:T(8,128)(2,1)} %scatter_fusion.1, bf16[128,16,2,16,128]{4,3,2,1,0:T(8,128)(2,1)} %gather_fusion.4), kind=kOutput, calls=%fused_computation.17 | convolution fusion | flops 1086259200 | bytes 38019072 | tf_op jit(solution)/shard_map/snkgd,ntkd->nksgt/dot_general | solution.py:71
  117.5 24.9 %fusion.3 = f32[128,2,16,16]{3,2,1,0:T(8,128)} fusion(f32[128,2,16,16,64]{4,3,2,1,0:T(8,128)} %get-tuple-element.35, f32[128,2,16,16]{3,2,1,0:T(8,128)S(1)} %get-tuple-element.34, pred[128,64]{1,0:T(8,128)(4,1)S(1)} %iota_compare_fusion), kind=kLoop, calls=%fused_computation.18 | loop fusion | flops 20905984 | bytes 17309696 | tf_op jit(solution)/shard_map/reduce_sum | solution.py:79
  143.3 38.4 %pmax.7 = f32[12,2,16,16]{3,2,1,0:T(8,128)S(1)} all-reduce(f32[12,2,16,16]{3,2,1,0:T(8,128)S(1)} %max.16), channel_id=1, replica_groups=mesh['inst'=8,'head'=4] {'inst'}, use_global_device_ids=true, to_apply=%region_10.11 | all-reduce | flops 6144 | bytes 49152 | tf_op jit(solution)/shard_map/pmax | solution.py:105
  183.9 5.1 %fusion.49 = (f32[128,2,16,16]{3,2,1,0:T(8,128)}, f32[128,2,16,16]{3,2,1,0:T(8,128)}) fusion(f32[128,2,16,16]{3,2,1,0:T(8,128)} %fusion.3, f32[128,2,16,16]{3,2,1,0:T(8,128)S(1)} %get-tuple-element.34, f32[128,2,16,16]{3,2,1,0:T(8,128)} %gather_fusion.5), kind=kLoop, calls=%fused_computation.83 | loop fusion | flops 131072 | bytes 1310720 | tf_op jit(solution)/shard_map/mul | solution.py:111
  191.7 26.3 %broadcast_multiply_fusion = f32[128,2,16,16,128]{4,3,2,1,0:T(8,128)} fusion(f32[128,2,16,16]{3,2,1,0:T(8,128)} %get-tuple-element.22, f32[128,2,16,16,64]{4,3,2,1,0:T(8,128)} %get-tuple-element.35, f32[128,2,16,16]{3,2,1,0:T(8,128)S(1)} %get-tuple-element.34, pred[128,64]{1,0:T(8,128)(4,1)S(1)} %iota_compare_fusion, ...), kind=kOutput, calls=%fused_computation.25 | convolution fusion | flops 1103101952 | bytes 55058432 | tf_op jit(solution)/shard_map/nksgt,ntkd->nksgd/dot_general | solution.py:80
  218.0 37.6 %fusion.23 = f32[16,12,2,16,128]{4,1,3,0,2:T(8,128)} fusion(f32[128,2,16,16,128]{4,3,2,1,0:T(8,128)} %broadcast_multiply_fusion, s32[128]{0:T(128)S(1)} %scatter_fusion.4), kind=kOutput, calls=%fused_computation.40 | convolution fusion | flops 1207961088 | bytes 36700672 | tf_op jit(solution)/shard_map/nr,nksgd->rksgd/dot_general | solution.py:107
  268.8 39.2 %psum.7 = f32[12,2,16,16]{3,2,1,0:T(8,128)} all-reduce(f32[12,2,16,16]{3,2,1,0:T(8,128)} %copy.147), channel_id=1, replica_groups=mesh['inst'=8,'head'=4] {'inst'}, use_global_device_ids=true, to_apply=%region_13.14 | all-reduce | flops 6144 | bytes 49152 | tf_op jit(solution)/shard_map/psum | solution.py:124
  318.6 18.3 %reduce-scatter.3.cloned.1.call-done = f32[16,12,512]{2,0,1:T(8,128)} async-done(((f32[16,12,4096]{2,0,1:T(8,128)}), f32[16,12,512]{2,0,1:T(8,128)}) %reduce-scatter.3.cloned.1.call-update) | async-done | bytes 393232 | tf_op jit(solution)/shard_map/reduce_scatter | solution.py:121
  339.5 44.7 %all-gather.2.cloned.1.call-done = bf16[16,12,4096]{2,0,1:T(8,128)(2,1)} async-done(((bf16[16,12,512]{2,0,1:T(8,128)(2,1)}), bf16[16,12,4096]{2,0,1:T(8,128)(2,1)}) %all-gather.2.cloned.1.call-update) | async-done | bytes 1572880 | tf_op jit(solution)/shard_map/all_gather | solution.py:133
  384.1 10.8 %fusion.7 = f32[16,12,2048]{2,0,1:T(8,128)} fusion(bf16[16,12,4096]{2,0,1:T(8,128)(2,1)} %all-gather.2.cloned.1.call-done, bf16[4096,2048]{1,0:T(8,128)(2,1)} %param.19), kind=kOutput, calls=%fused_computation.21 | convolution fusion | flops 3221225472 | bytes 19922944 | tf_op jit(solution)/shard_map/dot_general | solution.py:135
  395.0 12.8 %copy.150 = bf16[128,64,2,128]{3,2,1,0:T(2,128)(2,1)} copy(bf16[128,64,2,128]{3,1,2,0:T(8,128)(2,1)} %scatter_fusion.3) | data formatting | bytes 8388608
  407.8 10.6 %copy.149 = bf16[128,64,2,128]{3,2,1,0:T(2,128)(2,1)} copy(bf16[128,64,2,128]{3,1,2,0:T(8,128)(2,1)S(1)} %copy-done.3) | data formatting | bytes 8388608
  (82 shorter events, 50.4 us)
Async XLA Ops:
  7.2 302.6 %copy-start = (bf16[16,12,2,128]{3,2,1,0:T(2,128)(2,1)S(1)}, bf16[16,12,2,128]{3,2,1,0:T(2,128)(2,1)}, u32[]{:S(2)}) copy-start(bf16[16,12,2,128]{3,2,1,0:T(2,128)(2,1)} %param.18) | copy-start | bytes 294916
  20.2 11.6 %copy-start.8 = (s32[1,8,2]{1,2,0:T(2,128)S(1)}, s32[1,8,2]{1,2,0:T(2,128)}, u32[]{:S(2)}) copy-start(s32[1,8,2]{1,2,0:T(2,128)} %param.14) | copy-start | bytes 196
  20.2 13.2 %copy-start.9 = (s32[1,8,2]{1,2,0:T(2,128)S(1)}, s32[1,8,2]{1,2,0:T(2,128)}, u32[]{:S(2)}) copy-start(s32[1,8,2]{1,2,0:T(2,128)} %param.15) | copy-start | bytes 196
  34.2 17.6 %all-to-all-start = ((s32[8,2,3]{2,1,0:T(2,128)}), s32[8,2,3]{2,1,0:T(2,128)S(1)}, u32[]{:S(2)}, u32[]{:S(2)}) async-start(s32[8,2,3]{2,1,0:T(2,128)} %copy.132), calls=%async_computation | async-start | bytes 16384 | tf_op jit(solution)/shard_map/all_to_all | solution.py:45
  51.8 40.2 %all-to-all-start.1 = ((bf16[8,2,2,64,2,128]{5,4,3,1,2,0:T(2,128)(2,1)}), bf16[8,2,2,64,2,128]{5,4,3,1,2,0:T(2,128)(2,1)S(1)}, u32[]{:S(2)}, u32[]{:S(2)}) async-start(bf16[8,2,2,64,2,128]{5,4,3,1,2,0:T(2,128)(2,1)} %pad_maximum_fusion), calls=%async_computation.1 | async-start | bytes 2097152 | tf_op jit(solution)/shard_map/all_to_all | solution.py:44
  57.8 279.1 %reduce-scatter.3.cloned.1.call-start = ((), (), s32[]{:S(2)}) async-start(), calls=%async_computation.4 | async-start | bytes 3538944 | tf_op jit(solution)/shard_map/reduce_scatter | solution.py:121
  67.2 5.6 %copy-start.2 = (bf16[128,64,2,128]{3,2,1,0:T(2,128)(2,1)S(1)}, bf16[128,64,2,128]{3,2,1,0:T(2,128)(2,1)}, u32[]{:S(2)}) copy-start(bf16[128,64,2,128]{3,2,1,0:T(2,128)(2,1)} %scatter_fusion.2) | copy-start | bytes 12582916
  72.8 3.3 copy-start.1
  72.8 3.3 copy-start.10
  81.5 61.8 %copy-start.6 = (f32[12,2,16,16]{3,2,1,0:T(8,128)}, f32[12,2,16,16]{3,2,1,0:T(8,128)S(1)}, u32[]{:S(2)}) copy-start(f32[12,2,16,16]{3,2,1,0:T(8,128)S(1)} %get-tuple-element.32) | copy-start | bytes 73732
  261.2 1.9 copy-start.4
  261.2 122.9 %all-gather.2.cloned.1.call-start = ((), (), s32[]{:S(2)}) async-start(), calls=%async_computation.5 | async-start | bytes 1769472 | tf_op jit(solution)/shard_map/all_gather | solution.py:133
  261.3 4.8 %copy-start.5 = (f32[128,2,16,16]{3,2,1,0:T(8,128)S(1)}, f32[128,2,16,16]{3,2,1,0:T(8,128)}, u32[]{:S(2)}) copy-start(f32[128,2,16,16]{3,2,1,0:T(8,128)} %get-tuple-element.21) | copy-start | bytes 786436
  312.9 2.4 copy-start.7
  339.0 82.5 %reduce-scatter.5.cloned.1.call-start = ((), (), s32[]{:S(2)}) async-start(), calls=%async_computation.6 | async-start | bytes 1966080 | tf_op jit(solution)/shard_map/reduce_scatter | solution.py:138
  395.0 12.8 %copy-start.3 = (bf16[128,64,2,128]{3,1,2,0:T(8,128)(2,1)S(1)}, bf16[128,64,2,128]{3,1,2,0:T(8,128)(2,1)}, u32[]{:S(2)}) copy-start(bf16[128,64,2,128]{3,1,2,0:T(8,128)(2,1)} %scatter_fusion.1) | copy-start | bytes 12582916
Sparse Core Ops, SparseCore 0:
  261.4 75.5 reduce-scatter.2
  339.6 44.4 all-gather.1
  395.1 26.3 reduce-scatter.4
where the time goes:
time: 438 us; the launch traced here: 430 us
  local copies, waits for them, and re-layouts  110 us (25%)
  matrix products  106 us (24%)
  blocking collectives  77.6 us (18%)
  waiting for transfers between devices  66.1 us (15%)
  other arithmetic  42 us (10%)
  between operations  14.2 us (3%)
  starting transfers between devices  14.1 us (3%)
    unnamed x32, local copies, waits for them, and re-layouts  50.1 us
    all_gather x1, waiting for transfers between devices, shards(): lax.all_gather(share_part.astype(jnp.bfloat16), 'inst', axis=2, tiled=True)  44.7 us
    psum x1, blocking collectives, shards(): denominator_all = lax.psum(denominator, 'inst')  39.2 us
    pmax x1, blocking collectives, shards(): score_peak = lax.pmax(jnp.maximum(local_peak, fresh_peak), 'inst')  38.4 us
    dot_general x1, matrix products, shards(): jnp.einsum('nr,nksgd->rksgd', indicator, per_slot * factor[..., None], pr...  37.6 us
    dot_general x1, matrix products, shards(): jnp.einsum('nksgt,ntkd->nksgd', weights.astype(jnp.bfloat16), values, pre...  26.3 us
    reduce_sum x1, other arithmetic, shards(): weight_sum = weights.sum(-1)  24.9 us
    dot_general x1, matrix products, shards(): jnp.einsum('snkgd,ntkd->nksgt', chosen, keys, preferred_element_type=jnp....  21.3 us
  transfers between devices with their start and end apart: 5, of which 3 were waited for; matrix products, arithmetic and copies ran while one was open for 20% of the time, Pallas kernels for 0%

commit v1 on v0

--- a/solution.py
+++ b/solution.py
@@ -1,11 +1,31 @@
+import functools
 import math
 
 import jax
 import jax.numpy as jnp
 from jax import lax
+from jax.experimental import pallas as pl
+from jax.experimental.pallas import tpu as pltpu
 from jax.sharding import PartitionSpec as P
 
 masked_score = -1e30
+start_peak = -5e29
+GROUP = 4
+LEAD = 4
+VMEM = pl.BlockSpec(memory_space=pltpu.VMEM)
+SMEM = pl.BlockSpec(memory_space=pltpu.SMEM)
+ANY = pl.BlockSpec(memory_space=pl.ANY)
+f32, bf16 = jnp.float32, jnp.bfloat16
+
+
+def limit(mib):
+    return pltpu.CompilerParams(vmem_limit_bytes=mib * 2**20)
+
+
+def in_parts(x):
+    first = x.astype(bf16).astype(f32)
+    second = (x - first).astype(bf16).astype(f32)
+    return first, second, x - first - second
 
 
 def flatten_heads(values):
@@ -13,7 +33,7 @@
     return values.transpose(2, 0, 1, 3, 4).reshape(step_count, requests, -1)
 
 
-def shards(
+def general(
     cache_keys,
     cache_values,
     slot_req,
@@ -141,6 +161,473 @@
     return (moved_keys, moved_values, output)
 
 
+def attention_kernel(
+    req_ref, fill_ref, q_ref, k_vmem, v_vmem,
+    out_ref,
+    q_turned, k_wide, v_wide, k_ready, v_ready, scores, fresh_peak, weights, factor_ref,
+    peak, total, old_peak, old_total, acc, lse_acc,
+    order, order_fill, item_req, count,
+):
+    slots, rows, head_dim = k_vmem.shape
+    steps, requests, heads, _ = q_ref.shape
+    kv_local = q_turned.shape[1]
+    page = rows // kv_local
+    group = heads // kv_local
+    q_rows = steps * group
+    tokens = GROUP * page
+    f32, bf16 = jnp.float32, jnp.bfloat16
+    scale = math.log2(math.e) / math.sqrt(head_dim)
+    peers, chunk_rows, _ = out_ref.shape
+    near = steps // peers
+    body_rows = near * requests * heads
+
+    def clear(r, _):
+        count[r] = 0
+        return 0
+
+    lax.fori_loop(0, requests, clear, 0)
+
+    def tally(i, _):
+        r = req_ref[i]
+        count[r] = count[r] + (fill_ref[i] > 0).astype(jnp.int32)
+        return 0
+
+    lax.fori_loop(0, slots, tally, 0, unroll=8)
+    def blank(item, r):
+        item_req[item] = r
+        for g in range(GROUP):
+            order[item * GROUP + g] = 0
+            order_fill[item * GROUP + g] = 0
+    for item in range(LEAD):
+        blank(item, -1)
+
+    def place(r, item):
+        items = (count[r] + GROUP - 1) // GROUP
+        count[r] = item * GROUP
+        last = item + items - 1
+
+        @pl.when(items > 0)
+        def _():
+            blank(last, r)
+
+        def name(j, _):
+            item_req[j] = r
+            return 0
+
+        lax.fori_loop(item, last, name, 0)
+        return last + 1
+
+    end = lax.fori_loop(0, requests, place, LEAD)
+    for item in range(LEAD):
+        blank(end + item, -1)
+
+    def insert(i, _):
+        fill = fill_ref[i]
+
+        @pl.when(fill > 0)
+        def _():
+            r = req_ref[i]
+            at = count[r]
+            order[at] = i
+            order_fill[at] = fill
+            count[r] = at + 1
+
+        return 0
+
+    lax.fori_loop(0, slots, insert, 0, unroll=8)
+
+    def turn(r, _):
+        for k in range(kv_local):
+            q_turned[r, k] = q_ref[:, r, k * group : (k + 1) * group, :].reshape(q_rows, head_dim).T
+        return 0
+
+    lax.fori_loop(0, requests, turn, 0, unroll=2)
+    out_ref[...] = jnp.zeros_like(out_ref)
+    lse_acc[...] = jnp.full(lse_acc.shape, masked_score, f32)
+    for ref in (acc, weights, scores, peak, total, old_peak, old_total, fresh_peak, factor_ref, k_ready, v_ready):
+        ref[...] = jnp.zeros_like(ref)
+    token = lax.broadcasted_iota(jnp.int32, (page, q_rows), 0)
+
+    def finish(t):
+        r = item_req[t]
+
+        @pl.when((r >= 0) & (item_req[t + 1] != r))
+        def _():
+            for k in range(kv_local):
+                l = old_total[k].sum(axis=0, keepdims=True)
+                o = (acc[k] * (1.0 / l)).T
+                o = o.astype(bf16)
+                for s in range(steps):
+                    at = ((s % near) * requests + r) * heads + k * group
+                    out_ref[s // near, pl.ds(pl.multiple_of(at, group), group), :] = o[s * group : (s + 1) * group]
+                lse_acc[pl.ds(r * kv_local + k, 1), :] = old_peak[k, :1] + jnp.log2(l)
+
+    def collect(t):
+        for k in range(kv_local):
+            pv = jnp.dot(v_ready[k], weights[k], preferred_element_type=f32)
+            acc[k] = acc[k] * factor_ref[k, :1] + pv
+
+    def soften(t):
+        first = item_req[t] != item_req[t - 1]
+        for k in range(kv_local):
+            before = peak[k]
+            sums = total[k]
+            old_peak[k] = before
+            old_total[k] = sums
+            before = jnp.where(first, start_peak, before)
+            m = jnp.maximum(before, fresh_peak[k])
+            factor = jnp.exp2(before - m)
+            peak[k] = m
+            factor_ref[k] = factor
+            parts = []
+            add = jnp.zeros((8, q_rows), f32)
+            for a in range(0, tokens, 16):
+                p = [jnp.exp2(scores[k, b : b + 8] * scale - m) for b in (a, a + 8)]
+                add = add + (p[0] + p[1])
+                weights[k, a : a + 16] = jnp.concatenate(p, axis=0).astype(bf16)
+            total[k] = sums * factor + add
+
+    def score(t):
+        r = jnp.maximum(item_req[t], 0)
+        for k in range(kv_local):
+            s = jnp.dot(k_ready[k], q_turned[r, k], preferred_element_type=f32)
+            high = jnp.full((8, q_rows), -3e30, f32)
+            for g in range(GROUP):
+                part = jnp.where(token < order_fill[t * GROUP + g], s[g * page : (g + 1) * page], masked_score / scale)
+                scores[k, g * page : (g + 1) * page] = part
+                for a in range(0, page, 8):
+                    high = jnp.maximum(high, part[a : a + 8])
+            fresh_peak[k] = jnp.broadcast_to(high.max(axis=0, keepdims=True) * scale, (8, q_rows))
+
+    def ready(t, source, wide):
+        for g in range(GROUP):
+            wide[g * rows : (g + 1) * rows, :] = source[order[t * GROUP + g]].astype(f32)
+        for k in range(kv_local):
+            part = pl.ds(k, tokens, stride=kv_local) if kv_local > 1 else pl.ds(0, tokens)
+            yield k, wide[part, :].astype(bf16)
+
+    def step(t, _):
+        finish(t - 4)
+        collect(t - 3)
+        soften(t - 2)
+        score(t - 1)
+        for k, keys in ready(t, k_vmem, k_wide):
+            k_ready[k] = keys
+        for k, values in ready(t - 2, v_vmem, v_wide):
+            v_ready[k] = values.T
+        return 0
+
+    lax.fori_loop(LEAD, end + LEAD, step, 0)
+    first, second, third = in_parts(lse_acc[...].T)
+    lane = lax.broadcasted_iota(jnp.int32, (q_rows, head_dim), 1)
+    slot = head_dim // 4
+    packed = jnp.where(lane < slot, first, pltpu.roll(second, slot, 1))
+    packed = jnp.where(lane < 2 * slot, packed, pltpu.roll(third, 2 * slot, 1)).astype(bf16)
+    for j in range(peers):
+        out_ref[j, body_rows:, :] = packed[j * near * group : (j + 1) * near * group]
+
+
+def local_attention(keys, values, slot_req, slot_fill, queries, kv_local, peers):
+    slots, rows, head_dim = keys.shape
+    steps, requests, heads, _ = queries.shape
+    q_rows = steps * heads // kv_local
+    tokens = GROUP * rows // kv_local
+    items = slots // GROUP + requests + 2 * LEAD
+    stat = pltpu.VMEM((kv_local, 8, q_rows), f32)
+    chunk = steps // peers * (requests * heads + heads // kv_local)
+    return pl.pallas_call(
+        attention_kernel,
+        out_shape=jax.ShapeDtypeStruct((peers, chunk, head_dim), bf16),
+        in_specs=[SMEM, SMEM, VMEM, VMEM, VMEM],
+        out_specs=VMEM,
+        scratch_shapes=[
+            pltpu.VMEM((requests, kv_local, head_dim, q_rows), bf16),
+            pltpu.VMEM((GROUP * rows, head_dim), f32),
+            pltpu.VMEM((GROUP * rows, head_dim), f32),
+            pltpu.VMEM((kv_local, tokens, head_dim), bf16),
+            pltpu.VMEM((kv_local, head_dim, tokens), bf16),
+            pltpu.VMEM((kv_local, tokens, q_rows), f32),
+            stat,
+            pltpu.VMEM((kv_local, tokens, q_rows), bf16),
+            stat, stat, stat, stat, stat,
+            pltpu.VMEM((kv_local, head_dim, q_rows), f32),
+            pltpu.VMEM((head_dim, q_rows), f32),
+            pltpu.SMEM((items * GROUP,), jnp.int32),
+            pltpu.SMEM((items * GROUP,), jnp.int32),
+            pltpu.SMEM((items,), jnp.int32),
+            pltpu.SMEM((requests,), jnp.int32),
+        ],
+        compiler_params=limit(32),
+        cost_estimate=pl.CostEstimate(flops=3 * 10**9, bytes_accessed=2**24, transcendentals=10**7),
+    )(slot_req, slot_fill, queries, keys, values)
+
+
+def pack_kernel(src_ref, dst_ref, k_ref, v_ref, parcel_ref, label, sems):
+    peers, length, lanes = parcel_ref.shape
+    slots, rows, _ = k_ref.shape
+    capacity = src_ref.shape[0] // peers
+    copies = []
+    for j in range(peers):
+        for c in range(capacity):
+            n = jnp.maximum(src_ref[j * capacity + c], 0)
+            for i, ref in enumerate((k_ref, v_ref)):
+                a = i * capacity + c
+                copies.append(
+                    pltpu.make_async_copy(
+                        ref.at[n], parcel_ref.at[j, pl.ds(a * rows, rows)], sems.at[j, a]
+                    )
+                )
+                copies[-1].start()
+    lane = lax.broadcasted_iota(jnp.int32, label.shape[1:], 1)
+    for j in range(peers):
+        word = jnp.zeros(label.shape[1:], jnp.int32)
+        for c in range(capacity):
+            word = jnp.where(lane == c, dst_ref[j * capacity + c], word)
+        label[j] = word.astype(f32).astype(bf16)
+    body = 2 * capacity * rows
+    last = pltpu.make_async_copy(
+        label, parcel_ref.at[:, pl.ds(body, length - body)], sems.at[0, 2 * capacity]
+    )
+    last.start()
+    for copy in copies:
+        copy.wait()
+    last.wait()
+
+
+def pack(keys, values, outgoing, landing, peers):
+    slots, rows, lanes = keys.shape
+    capacity = outgoing.shape[0] // peers
+    return pl.pallas_call(
+        pack_kernel,
+        out_shape=jax.ShapeDtypeStruct((peers, 2 * capacity * rows + 16, lanes), bf16),
+        in_specs=[SMEM, SMEM, ANY, ANY],
+        out_specs=ANY,
+        scratch_shapes=[
+            pltpu.VMEM((peers, 16, lanes), bf16),
+            pltpu.SemaphoreType.DMA((peers, 2 * capacity + 1)),
+        ],
+    )(outgoing, landing, keys, values)
+
+
+def place_kernel(src_ref, target_ref, k_ref, v_ref, arrived_ref, mk_ref, mv_ref, blank, sems, page_sems, zero_sems):
+    slots, rows, _ = k_ref.shape
+    peers = arrived_ref.shape[0]
+    capacity = src_ref.shape[0] // peers
+    parts = sems.shape[1]
+    per = slots // parts
+    copies = []
+    for p in range(parts):
+        for i, (a, b) in enumerate(((k_ref, mk_ref), (v_ref, mv_ref))):
+            part = pl.ds(p * per, per)
+            copies.append(pltpu.make_async_copy(a.at[part], b.at[part], sems.at[i, p]))
+            copies[-1].start()
+    blank[...] = jnp.zeros_like(blank)
+    for copy in copies:
+        copy.wait()
+
+    def each(act):
+        for i, ref in enumerate((mk_ref, mv_ref)):
+            for j in range(peers):
+                for c in range(capacity):
+                    leaving = src_ref[j * capacity + c]
+                    taken = target_ref[j * capacity + c]
+
+                    @pl.when(leaving >= 0)
+                    def _():
+                        act(pltpu.make_async_copy(blank, ref.at[leaving], zero_sems.at[i, j, c]))
+
+                    @pl.when(taken >= 0)
+                    def _():
+                        part = pl.ds((i * capacity + c) * rows, rows)
+                        act(pltpu.make_async_copy(arrived_ref.at[j, part], ref.at[taken], page_sems.at[i, j, c]))
+
+    each(lambda copy: copy.start())
+    each(lambda copy: copy.wait())
+
+
+def place(keys, values, arrived, outgoing, target):
+    slots, rows, lanes = keys.shape
+    peers = arrived.shape[0]
+    capacity = outgoing.shape[0] // peers
+    each = pltpu.SemaphoreType.DMA((2, peers, capacity))
+    return pl.pallas_call(
+        place_kernel,
+        out_shape=(jax.ShapeDtypeStruct(keys.shape, bf16),) * 2,
+        in_specs=[SMEM, SMEM, ANY, ANY, ANY],
+        out_specs=(ANY, ANY),
+        scratch_shapes=[
+            pltpu.VMEM((rows, lanes), bf16),
+            pltpu.SemaphoreType.DMA((2, 8)),
+            each,
+            each,
+        ],
+        cost_estimate=pl.CostEstimate(flops=0, bytes_accessed=2**25, transcendentals=0),
+    )(outgoing, target, keys, values, arrived)
+
+
+def fresh_kernel(q_ref, nk_ref, nv_ref, mine_ref, out_ref, lse_ref, *, kv_local):
+    near, requests, heads, head_dim = q_ref.shape
+    steps = nk_ref.shape[0]
+    group = heads // kv_local
+    rows = near * group
+    scale = math.log2(math.e) / math.sqrt(head_dim)
+    step = lax.broadcasted_iota(jnp.int32, (rows, steps), 0) // group + mine_ref[0] * near
+    live = lax.broadcasted_iota(jnp.int32, (rows, steps), 1) <= step
+    lane = lax.broadcasted_iota(jnp.int32, (rows, head_dim), 1)
+    lse = jnp.zeros((rows, head_dim), f32)
+    for r in range(requests):
+        for k in range(kv_local):
+            n = r * kv_local + k
+            q = q_ref[:, r, k * group : (k + 1) * group, :].reshape(rows, head_dim)
+            s = lax.dot_general(q, nk_ref[:, n, :].astype(bf16), (((1,), (1,)), ((), ())), preferred_element_type=f32)
+            s = jnp.where(live, s * scale, masked_score)
+            m = s.max(axis=1, keepdims=True)
+            p = jnp.exp2(s - m)
+            l = p.sum(axis=1, keepdims=True)
+            o = jnp.dot(p.astype(bf16), nv_ref[:, n, :].astype(bf16), preferred_element_type=f32) * (1.0 / l)
+            out_ref[:, r, k * group : (k + 1) * group, :] = o.reshape(near, group, head_dim)
+            lse = jnp.where(lane == n, m + jnp.log2(l), lse)
+    lse_ref[...] = lse
+
+
+def fresh_part(queries, new_keys, new_values, mine, kv_local):
+    near, requests, heads, head_dim = queries.shape
+    steps = new_keys.shape[0]
+    wide = (steps, requests * kv_local, head_dim)
+    return pl.pallas_call(
+        functools.partial(fresh_kernel, kv_local=kv_local),
+        out_shape=(
+            jax.ShapeDtypeStruct(queries.shape, f32),
+            jax.ShapeDtypeStruct((near * heads // kv_local, head_dim), f32),
+        ),
+        in_specs=[VMEM, VMEM, VMEM, SMEM],
+        out_specs=(VMEM, VMEM),
+        compiler_params=limit(16),
+        cost_estimate=pl.CostEstimate(flops=10**8, bytes_accessed=2**21, transcendentals=10**5),
+    )(queries, new_keys.astype(f32).reshape(wide), new_values.astype(f32).reshape(wide), mine)
+
+
+def combine_kernel(parts_ref, fresh_ref, fresh_lse_ref, out_ref, rows_ref, *, kv_local):
+    peers = parts_ref.shape[0]
+    near, requests, heads, head_dim = fresh_ref.shape
+    group = heads // kv_local
+    body = near * requests * heads
+    slot = head_dim // 4
+    peaks = [fresh_lse_ref[...]]
+    for i in range(peers):
+        x = parts_ref[i, body:, :].astype(f32)
+        peaks.append(x + pltpu.roll(x, head_dim - slot, 1) + pltpu.roll(x, head_dim - 2 * slot, 1))
+    top = functools.reduce(jnp.maximum, peaks)
+    shares = [jnp.exp2(x - top) for x in peaks]
+    whole = 1.0 / functools.reduce(jnp.add, shares)
+    shares = [x * whole for x in shares]
+    for r in range(requests):
+        for k in range(kv_local):
+            n = r * kv_local + k
+            cols = [x[:, n : n + 1] for x in shares]
+            o = fresh_ref[:, r, k * group : (k + 1) * group, :].reshape(near * group, head_dim) * cols[0]
+            for i in range(peers):
+                part = [
+                    parts_ref[i, pl.ds((s * requests + r) * heads + k * group, group), :].astype(f32)
+                    for s in range(near)
+                ]
+                o = o + jnp.concatenate(part, axis=0) * cols[i + 1]
+            for s in range(near):
+                rows_ref[pl.ds((s * requests + r) * heads + k * group, group), :] = o[s * group : (s + 1) * group]
+    for h in range(heads):
+        out_ref[:, h * head_dim : (h + 1) * head_dim] = rows_ref[pl.ds(h, near * requests, stride=heads), :].astype(bf16)
+
+
+def combine(parts, fresh, fresh_lse, kv_local):
+    near, requests, heads, head_dim = fresh.shape
+    return pl.pallas_call(
+        functools.partial(combine_kernel, kv_local=kv_local),
+        out_shape=jax.ShapeDtypeStruct((near * requests, heads * head_dim), bf16),
+        in_specs=[VMEM] * 3,
+        out_specs=VMEM,
+        scratch_shapes=[pltpu.VMEM((near * requests * heads, head_dim), f32)],
+        compiler_params=limit(16),
+    )(parts, fresh, fresh_lse)
+
+
+def project_kernel(mine_ref, *refs, sides):
+    blocks, (w_ref, out_ref, rows_ref, sums_ref) = refs[:-4], refs[-4:]
+    rows = blocks[0].shape[0]
+    for i, block in enumerate(blocks):
+        rows_ref[i * rows : (i + 1) * rows, :] = block[...].astype(f32)
+    width = w_ref.shape[1] // sides
+    x = rows_ref[...].astype(bf16)
+    for b in range(sides):
+        sums_ref[b] = jnp.dot(x, w_ref[:, b * width : (b + 1) * width], preferred_element_type=f32)
+    for p in range(sides):
+        out_ref[p] = sums_ref[p ^ mine_ref[0]].astype(bf16)
+
+
+def project(blocks, weight, mine, sides):
+    rows, depth = blocks[0].shape
+    rows *= len(blocks)
+    width = weight.shape[1] // sides
+    return pl.pallas_call(
+        functools.partial(project_kernel, sides=sides),
+        out_shape=jax.ShapeDtypeStruct((sides, rows, width), bf16),
+        in_specs=[SMEM] + [VMEM] * (len(blocks) + 1),
+        out_specs=VMEM,
+        scratch_shapes=[pltpu.VMEM((rows, depth), f32), pltpu.VMEM((sides, rows, width), f32)],
+        compiler_params=limit(40),
+    )(mine, *blocks, weight)
+
+
+def mirrored(axis, k):
+    return [(i, i ^ k) for i in range(lax.axis_size(axis))]
+
+
+def gather_over(x, axis):
+    count = lax.axis_size(axis)
+    got = {0: x}
+    for k in range(2, count, 2):
+        got[k] = lax.ppermute(x, axis, mirrored(axis, k))
+    for k in range(0, count, 2):
+        got[k + 1] = lax.ppermute(got[k], axis, mirrored(axis, 1))
+    return [got[k] for k in range(count)]
+
+
+def shards(cache_keys, cache_values, slot_req, slot_fill, mig_src, mig_dst, queries, new_keys, new_values, out_weight):
+    slots, page, kv_local, head_dim = cache_keys.shape
+    steps, requests, heads, _ = queries.shape
+    peers, sides = lax.axis_size("inst"), lax.axis_size("head")
+    if steps % peers or sides != 4 or peers & (peers - 1) or slots > 256:
+        return general(
+            cache_keys, cache_values, slot_req, slot_fill, mig_src, mig_dst, queries, new_keys, new_values, out_weight
+        )
+    near = steps // peers
+    me = lax.axis_index("inst")
+    mine = me.reshape(1).astype(jnp.int32)
+    side = lax.axis_index("head").reshape(1).astype(jnp.int32)
+    rows = page * kv_local
+    capacity = mig_src.shape[2]
+    keys = cache_keys.reshape(slots, rows, head_dim)
+    values = cache_values.reshape(slots, rows, head_dim)
+    outgoing, landing = mig_src.reshape(-1), mig_dst.reshape(-1)
+    parcel = pack(keys, values, outgoing, landing, peers)
+    arrived = lax.all_to_all(parcel, "inst", split_axis=0, concat_axis=0, tiled=True)
+    target = arrived[:, 2 * capacity * rows, :capacity].astype(jnp.int32).reshape(-1)
+    moved_keys, moved_values = place(keys, values, arrived, outgoing, target)
+
+    parts = local_attention(keys, values, slot_req, slot_fill, queries, kv_local, peers)
+    parts = lax.all_to_all(parts, "inst", split_axis=0, concat_axis=0, tiled=True)
+    own = lax.dynamic_slice_in_dim(queries, me * near, near, 0)
+    fresh, fresh_lse = fresh_part(own, new_keys, new_values, mine, kv_local)
+    blocks = gather_over(combine(parts, fresh, fresh_lse, kv_local), "inst")
+    shares = project(blocks, out_weight, side, sides)
+    lent = lax.ppermute(jnp.stack([shares[1], shares[3]]), "head", mirrored("head", 1))
+    kept = shares[0].astype(f32) + lent[0].astype(f32)
+    passed = (shares[2].astype(f32) + lent[1].astype(f32)).astype(bf16)
+    total = kept + lax.ppermute(passed, "head", mirrored("head", 2)).astype(f32)
+    total = total.astype(bf16).reshape(peers, near, requests, -1)
+    output = jnp.take(total, jnp.arange(peers) ^ me, axis=0).reshape(steps, requests, -1)
+    return moved_keys.reshape(cache_keys.shape), moved_values.reshape(cache_values.shape), output
+
+
 def solution(mesh):
     in_specs = (
         P("inst", None, "head", None),

time: 438 us -> 418 us (0.954); the launches traced: 430 us -> 418 us
  Pallas kernels: 0 us -> 332 us
  matrix products: 106 us -> 0 us
  local copies, waits for them, and re-layouts: 110 us -> 11.3 us
  blocking collectives: 77.6 us -> 0 us
  other arithmetic: 42 us -> 1.04 us
  waiting for transfers between devices: 66.1 us -> 45 us
  between operations: 14.2 us -> 0.83 us
  starting transfers between devices: 14.1 us -> 27.4 us
    pallas_call x0 -> x6, Pallas kernels: none -> 332 us  [the longest x1 274 us: place(): pl.pallas_call(place_kernel, out_shape=(jax.ShapeDtypeStruct(keys.shape,...]
    dot_general x7 -> x0, matrix products: 106 us -> none  [the longest x1 37.6 us: shards(): jnp.einsum('nr,nksgd->rksgd', indicator, per_slot * factor[..., None], pr...]
    all_gather x1 -> x0, waiting for transfers between devices: 44.7 us -> none  [shards(): lax.all_gather(share_part.astype(jnp.bfloat16), 'inst', axis=2, tiled=True)]
    unnamed x32 -> x22, local copies, waits for them, and re-layouts: 50.1 us -> 7.54 us
    ppermute x0 -> x9, waiting for transfers between devices: none -> 42 us  [the longest x3 32.6 us: gather_over(): got[k] = lax.ppermute(x, axis, mirrored(axis, k))]
    psum x1 -> x0, blocking collectives: 39.2 us -> none  [shards(): denominator_all = lax.psum(denominator, 'inst')]
    pmax x1 -> x0, blocking collectives: 38.4 us -> none  [shards(): score_peak = lax.pmax(jnp.maximum(local_peak, fresh_peak), 'inst')]
    reduce_sum x2 -> x0, other arithmetic: 27.9 us -> none  [the longest x1 24.9 us: shards(): weight_sum = weights.sum(-1)]
  transfers between devices with their start and end apart: 5 -> 11, of which waited for: 3 -> 6; matrix products, arithmetic and copies ran while one was open for 20% -> 1% of each run, Pallas kernels for 0% -> 76%
where the time goes in v1:
time: 418 us
  Pallas kernels  332 us (79%)
  waiting for transfers between devices  45 us (11%)
  starting transfers between devices  27.4 us (7%)
  local copies, waits for them, and re-layouts  11.3 us (3%)
    pallas_call x1, Pallas kernels, place(): pl.pallas_call(place_kernel, out_shape=(jax.ShapeDtypeStruct(keys.shape,...  274 us
    pallas_call x1, Pallas kernels, pack(): pl.pallas_call(pack_kernel, out_shape=jax.ShapeDtypeStruct((peers, 2 * ca...  33.9 us
    ppermute x3, waiting for transfers between devices, gather_over(): got[k] = lax.ppermute(x, axis, mirrored(axis, k))  32.6 us
    pallas_call x1, Pallas kernels, local_attention(): pl.pallas_call(attention_kernel, out_shape=jax.ShapeDtypeStruct((peers, c...  13.6 us
    all_to_all x1, starting transfers between devices, shards(): lax.all_to_all(parts, 'inst', split_axis=0, concat_axis=0, tiled=True)  12.1 us
    pallas_call x1, Pallas kernels, project(): pl.pallas_call(functools.partial(project_kernel, sides=sides), out_shape=...  9.26 us
  transfers between devices with their start and end apart: 11, of which 6 were waited for; matrix products, arithmetic and copies ran while one was open for 1% of the time, Pallas kernels for 76%

profile of v1, /device:TPU:0, one launch (start us, length us, event | category | flops | bytes accessed | tf_op | source)
XLA Modules:
  0.0 417.8 jit_solution(17913665749412018771)
XLA Ops:
  0.6 2.2 copy-done
  2.8 2.2 copy-done.1
  5.0 1.4 copy-done.2
  7.7 13.6 %shard_map.123 = bf16[8,800,128]{2,1,0:T(8,128)(2,1)} custom-call(s32[128]{0:T(128)S(1)} %copy-done.3, s32[128]{0:T(128)S(1)} %copy-done.4, bf16[16,12,32,128]{3,2,1,0:T(8,128)(2,1)S(1)} %copy-done.2, bf16[128,128,128]{2,1,0:T(8,128)(2,1)S(1)} %bitcast.21, bf16[128,128,128]{2,1,0:T(8,128)(2,1)S(1)} %bitcast.24), custom_call_target="tpu_custom_call" | custom-call | flops 3000000000 | bytes 16777216 | tf_op jit(solution)/shard_map/pallas_call | solution.py:338
  21.3 12.1 %all-to-all-start.1 = ((bf16[8,800,128]{2,1,0:T(8,128)(2,1)}), bf16[8,800,128]{2,1,0:T(8,128)(2,1)S(1)}, u32[]{:S(2)}, u32[]{:S(2)}) async-start(bf16[8,800,128]{2,1,0:T(8,128)(2,1)} %shard_map.123), calls=%async_computation.1 | async-start | bytes 3276800 | tf_op jit(solution)/shard_map/all_to_all | solution.py:617
  34.9 33.9 %shard_map.121 = bf16[8,528,128]{2,1,0:T(8,128)(2,1)} custom-call(s32[16]{0:T(128)} %reshape.78.src_ref, s32[16]{0:T(128)} %reshape.79.dst_ref, bf16[128,128,128]{2,1,0:T(8,128)(2,1)} %bitcast.19, bf16[128,128,128]{2,1,0:T(8,128)(2,1)} %bitcast.22), custom_call_target="tpu_custom_call" | custom-call | tf_op jit(solution)/shard_map/pallas_call | solution.py:400
  68.8 3.1 all-to-all-done.1.parts_ref
  71.9 3.6 all-to-all-start
  75.6 0.9 constant_dynamic-slice_fusion.q_ref
  76.5 0.7 shard_map.124
  77.3 1.2 shard_map.125.refs_0_
  78.5 3.9 collective-permute-start.5
  83.0 1.9 collective-permute-start
  85.0 17.8 %collective-permute-done.5.refs_6_ = bf16[24,4096]{1,0:T(8,128)(2,1)S(1)} collective-permute-done((bf16[24,4096]{1,0:T(8,128)(2,1)S(1)}, bf16[24,4096]{1,0:T(8,128)(2,1)S(1)}, u32[]{:S(2)}, u32[]{:S(2)}) %collective-permute-start.5) | collective-permute-done | bytes 196640 | tf_op jit(solution)/shard_map/ppermute | solution.py:588
  102.8 1.5 collective-permute-start.6
  104.3 14.7 %collective-permute-done.3.refs_4_ = bf16[24,4096]{1,0:T(8,128)(2,1)S(1)} collective-permute-done((bf16[24,4096]{1,0:T(8,128)(2,1)S(1)}, bf16[24,4096]{1,0:T(8,128)(2,1)S(1)}, u32[]{:S(2)}, u32[]{:S(2)}) %collective-permute-start.3) | collective-permute-done | bytes 196640 | tf_op jit(solution)/shard_map/ppermute | solution.py:588
  119.0 1.4 collective-permute-start.4
  121.0 5.8 %collective-permute-done.4.refs_5_ = bf16[24,4096]{1,0:T(8,128)(2,1)S(1)} collective-permute-done((bf16[24,4096]{1,0:T(8,128)(2,1)S(1)}, bf16[24,4096]{1,0:T(8,128)(2,1)S(1)}, u32[]{:S(2)}, u32[]{:S(2)}) %collective-permute-start.4) | collective-permute-done | bytes 196640 | tf_op jit(solution)/shard_map/ppermute | solution.py:590
  126.8 2.1 collective-permute-done.2.refs_3_
  128.9 9.3 %shard_map.126 = bf16[4,192,512]{2,1,0:T(8,128)(2,1)S(1)} custom-call(s32[1]{0:T(128)} %bitcast.4.mine_ref, bf16[24,4096]{1,0:T(8,128)(2,1)S(1)} %shard_map.125.refs_0_, bf16[24,4096]{1,0:T(8,128)(2,1)S(1)} %collective-permute-done.refs_1_, bf16[24,4096]{1,0:T(8,128)(2,1)S(1)} %collective-permute-done.1.refs_2_, ...), custom_call_target="tpu_custom_call" | custom-call | tf_op jit(solution)/shard_map/pallas_call | solution.py:570
  138.5 1.5 collective-permute-done.7
  140.1 1.6 collective-permute-start.8
  142.7 273.6 %shard_map.122 = (bf16[128,128,128]{2,1,0:T(8,128)(2,1)}, bf16[128,128,128]{2,1,0:T(8,128)(2,1)}) custom-call(s32[16]{0:T(128)} %reshape.78.src_ref, s32[16]{0:T(128)} %reshape.91.target_ref, bf16[128,128,128]{2,1,0:T(8,128)(2,1)} %bitcast.20, bf16[128,128,128]{2,1,0:T(8,128)(2,1)} %bitcast.23, bf16[8,528,128]{2,1,0:T(8,128)(2,1)} %copy-done.5), custom_call_target="tpu_custom_call" | custom-call | bytes 33554432 | tf_op jit(solution)/shard_map/pallas_call | solution.py:453
  417.0 0.8 copy_select_fusion
  (45 shorter events, 6.1 us)
Async XLA Ops:
  0.6 2.2 copy-start
  2.8 2.2 copy-start.1
  5.0 1.4 copy-start.2
  6.4 0.7 copy-start.3
  7.1 0.7 copy-start.4
  21.3 12.2 %copy-start.8 = (s32[1,8,2]{1,2,0:T(2,128)S(1)}, s32[1,8,2]{1,2,0:T(2,128)}, u32[]{:S(2)}) copy-start(s32[1,8,2]{1,2,0:T(2,128)} %param.14) | copy-start | bytes 196
  21.3 12.8 %copy-start.9 = (s32[1,8,2]{1,2,0:T(2,128)S(1)}, s32[1,8,2]{1,2,0:T(2,128)}, u32[]{:S(2)}) copy-start(s32[1,8,2]{1,2,0:T(2,128)} %param.15) | copy-start | bytes 196
  21.3 50.6 %all-to-all-start.1 = ((bf16[8,800,128]{2,1,0:T(8,128)(2,1)}), bf16[8,800,128]{2,1,0:T(8,128)(2,1)S(1)}, u32[]{:S(2)}, u32[]{:S(2)}) async-start(bf16[8,800,128]{2,1,0:T(8,128)(2,1)} %shard_map.123), calls=%async_computation.1 | async-start | bytes 3276800 | tf_op jit(solution)/shard_map/all_to_all | solution.py:617
  68.8 6.7 %copy-start.6 = (bf16[16,12,2,128]{3,2,1,0:T(2,128)(2,1)S(1)}, bf16[16,12,2,128]{3,2,1,0:T(2,128)(2,1)}, u32[]{:S(2)}) copy-start(bf16[16,12,2,128]{3,2,1,0:T(2,128)(2,1)} %param.17) | copy-start | bytes 294916
  68.8 6.7 %copy-start.7 = (bf16[16,12,2,128]{3,2,1,0:T(2,128)(2,1)S(1)}, bf16[16,12,2,128]{3,2,1,0:T(2,128)(2,1)}, u32[]{:S(2)}) copy-start(bf16[16,12,2,128]{3,2,1,0:T(2,128)(2,1)} %param.18) | copy-start | bytes 294916
  71.9 69.8 %all-to-all-start = ((bf16[8,528,128]{2,1,0:T(8,128)(2,1)}), bf16[8,528,128]{2,1,0:T(8,128)(2,1)S(1)}, u32[]{:S(2)}, u32[]{:S(2)}) async-start(bf16[8,528,128]{2,1,0:T(8,128)(2,1)} %shard_map.121), calls=%async_computation | async-start | bytes 2162688 | tf_op jit(solution)/shard_map/all_to_all | solution.py:612
  78.5 24.3 %collective-permute-start.5 = (bf16[24,4096]{1,0:T(8,128)(2,1)S(1)}, bf16[24,4096]{1,0:T(8,128)(2,1)S(1)}, u32[]{:S(2)}, u32[]{:S(2)}) collective-permute-start(bf16[24,4096]{1,0:T(8,128)(2,1)S(1)} %shard_map.125.refs_0_), channel_id=1, source_target_pairs={{0,24},{4,28},{8,16},{12,20},{16,8},{20,12},{24,0},{28,4},{1,25},{... | collective-permute-start | bytes 589832 | tf_op jit(solution)/shard_map/ppermute | solution.py:588
  82.4 36.6 %collective-permute-start.3 = (bf16[24,4096]{1,0:T(8,128)(2,1)S(1)}, bf16[24,4096]{1,0:T(8,128)(2,1)S(1)}, u32[]{:S(2)}, u32[]{:S(2)}) collective-permute-start(bf16[24,4096]{1,0:T(8,128)(2,1)S(1)} %shard_map.125.refs_0_), channel_id=1, source_target_pairs={{0,16},{4,20},{8,24},{12,28},{16,0},{20,4},{24,8},{28,12},{1,17},{... | collective-permute-start | bytes 589832 | tf_op jit(solution)/shard_map/ppermute | solution.py:588
  82.4 38.0 %collective-permute-start.1 = (bf16[24,4096]{1,0:T(8,128)(2,1)S(1)}, bf16[24,4096]{1,0:T(8,128)(2,1)S(1)}, u32[]{:S(2)}, u32[]{:S(2)}) collective-permute-start(bf16[24,4096]{1,0:T(8,128)(2,1)S(1)} %shard_map.125.refs_0_), channel_id=1, source_target_pairs={{0,8},{4,12},{8,0},{12,4},{16,24},{20,28},{24,16},{28,20},{1,9},{5... | collective-permute-start | bytes 589832 | tf_op jit(solution)/shard_map/ppermute | solution.py:588
  83.0 38.0 %collective-permute-start = (bf16[24,4096]{1,0:T(8,128)(2,1)S(1)}, bf16[24,4096]{1,0:T(8,128)(2,1)S(1)}, u32[]{:S(2)}, u32[]{:S(2)}) collective-permute-start(bf16[24,4096]{1,0:T(8,128)(2,1)S(1)} %shard_map.125.refs_0_), channel_id=1, source_target_pairs={{0,4},{4,0},{8,12},{12,8},{16,20},{20,16},{24,28},{28,24},{1,5},{5... | collective-permute-start | bytes 589832 | tf_op jit(solution)/shard_map/ppermute | solution.py:590
  102.8 18.2 %collective-permute-start.6 = (bf16[24,4096]{1,0:T(8,128)(2,1)S(1)}, bf16[24,4096]{1,0:T(8,128)(2,1)S(1)}, u32[]{:S(2)}, u32[]{:S(2)}) collective-permute-start(bf16[24,4096]{1,0:T(8,128)(2,1)S(1)} %collective-permute-done.5.refs_6_), channel_id=1, source_target_pairs={{0,4},{4,0},{8,12},{12,8},{16,20},{20,16},{24,28},{28,24},{1,5},{5... | collective-permute-start | bytes 589832 | tf_op jit(solution)/shard_map/ppermute | solution.py:590
  119.0 7.8 %collective-permute-start.4 = (bf16[24,4096]{1,0:T(8,128)(2,1)S(1)}, bf16[24,4096]{1,0:T(8,128)(2,1)S(1)}, u32[]{:S(2)}, u32[]{:S(2)}) collective-permute-start(bf16[24,4096]{1,0:T(8,128)(2,1)S(1)} %collective-permute-done.3.refs_4_), channel_id=1, source_target_pairs={{0,4},{4,0},{8,12},{12,8},{16,20},{20,16},{24,28},{28,24},{1,5},{5... | collective-permute-start | bytes 589832 | tf_op jit(solution)/shard_map/ppermute | solution.py:590
  120.4 8.5 %collective-permute-start.2 = (bf16[24,4096]{1,0:T(8,128)(2,1)S(1)}, bf16[24,4096]{1,0:T(8,128)(2,1)S(1)}, u32[]{:S(2)}, u32[]{:S(2)}) collective-permute-start(bf16[24,4096]{1,0:T(8,128)(2,1)S(1)} %collective-permute-done.1.refs_2_), channel_id=1, source_target_pairs={{0,4},{4,0},{8,12},{12,8},{16,20},{20,16},{24,28},{28,24},{1,5},{5... | collective-permute-start | bytes 589832 | tf_op jit(solution)/shard_map/ppermute | solution.py:590
  138.3 1.8 collective-permute-start.7
  140.1 276.2 %collective-permute-start.8 = (bf16[192,512]{1,0:T(8,128)(2,1)S(1)}, bf16[192,512]{1,0:T(8,128)(2,1)S(1)}, u32[]{:S(2)}, u32[]{:S(2)}) collective-permute-start(bf16[192,512]{1,0:T(8,128)(2,1)S(1)} %fusion.1), channel_id=1, source_target_pairs={{0,2},{1,3},{2,0},{3,1},{4,6},{5,7},{6,4},{7,5},{8,10},{9,11},{10,... | collective-permute-start | bytes 589832 | tf_op jit(solution)/shard_map/ppermute | solution.py:625
  141.7 1.0 copy-start.5

commit v2 on v1

--- a/solution.py
+++ b/solution.py
@@ -162,11 +162,11 @@
 
 
 def attention_kernel(
-    req_ref, fill_ref, q_ref, k_vmem, v_vmem,
-    out_ref,
-    q_turned, k_wide, v_wide, k_ready, v_ready, scores, fresh_peak, weights, factor_ref,
+    req_ref, fill_ref, q_ref, k_hbm, v_hbm,
+    out_ref, mk_hbm, mv_hbm,
+    k_vmem, v_vmem, q_turned, k_wide, v_wide, k_ready, v_ready, scores, fresh_peak, weights, factor_ref,
     peak, total, old_peak, old_total, acc, lse_acc,
-    order, order_fill, item_req, count,
+    order, order_fill, item_req, count, sems,
 ):
     slots, rows, head_dim = k_vmem.shape
     steps, requests, heads, _ = q_ref.shape
@@ -177,6 +177,10 @@
     tokens = GROUP * page
     f32, bf16 = jnp.float32, jnp.bfloat16
     scale = math.log2(math.e) / math.sqrt(head_dim)
+    loads = [pltpu.make_async_copy(*x) for x in ((k_hbm, k_vmem, sems.at[0]), (v_hbm, v_vmem, sems.at[1]))]
+    stores = [pltpu.make_async_copy(*x) for x in ((k_vmem, mk_hbm, sems.at[2]), (v_vmem, mv_hbm, sems.at[3]))]
+    for copy in loads:
+        copy.start()
     peers, chunk_rows, _ = out_ref.shape
     near = steps // peers
     body_rows = near * requests * heads
@@ -247,6 +251,9 @@
     for ref in (acc, weights, scores, peak, total, old_peak, old_total, fresh_peak, factor_ref, k_ready, v_ready):
         ref[...] = jnp.zeros_like(ref)
     token = lax.broadcasted_iota(jnp.int32, (page, q_rows), 0)
+    for load, store in zip(loads, stores):
+        load.wait()
+        store.start()
 
     def finish(t):
         r = item_req[t]
@@ -325,6 +332,8 @@
     packed = jnp.where(lane < 2 * slot, packed, pltpu.roll(third, 2 * slot, 1)).astype(bf16)
     for j in range(peers):
         out_ref[j, body_rows:, :] = packed[j * near * group : (j + 1) * near * group]
+    for store in stores:
+        store.wait()
 
 
 def local_attention(keys, values, slot_req, slot_fill, queries, kv_local, peers):
@@ -337,10 +346,16 @@
     chunk = steps // peers * (requests * heads + heads // kv_local)
     return pl.pallas_call(
         attention_kernel,
-        out_shape=jax.ShapeDtypeStruct((peers, chunk, head_dim), bf16),
-        in_specs=[SMEM, SMEM, VMEM, VMEM, VMEM],
-        out_specs=VMEM,
+        out_shape=(
+            jax.ShapeDtypeStruct((peers, chunk, head_dim), bf16),
+            jax.ShapeDtypeStruct(keys.shape, bf16),
+            jax.ShapeDtypeStruct(keys.shape, bf16),
+        ),
+        in_specs=[SMEM, SMEM, VMEM, ANY, ANY],
+        out_specs=(VMEM, ANY, ANY),
         scratch_shapes=[
+            pltpu.VMEM(keys.shape, bf16),
+            pltpu.VMEM(keys.shape, bf16),
             pltpu.VMEM((requests, kv_local, head_dim, q_rows), bf16),
             pltpu.VMEM((GROUP * rows, head_dim), f32),
             pltpu.VMEM((GROUP * rows, head_dim), f32),
@@ -356,13 +371,14 @@
             pltpu.SMEM((items * GROUP,), jnp.int32),
             pltpu.SMEM((items,), jnp.int32),
             pltpu.SMEM((requests,), jnp.int32),
+            pltpu.SemaphoreType.DMA((4,)),
         ],
-        compiler_params=limit(32),
+        compiler_params=limit(56),
         cost_estimate=pl.CostEstimate(flops=3 * 10**9, bytes_accessed=2**24, transcendentals=10**7),
     )(slot_req, slot_fill, queries, keys, values)
 
 
-def pack_kernel(src_ref, dst_ref, k_ref, v_ref, parcel_ref, label, sems):
+def pack_kernel(src_ref, dst_ref, k_ref, v_ref, parcel_ref, sems):
     peers, length, lanes = parcel_ref.shape
     slots, rows, _ = k_ref.shape
     capacity = src_ref.shape[0] // peers
@@ -378,20 +394,15 @@
                     )
                 )
                 copies[-1].start()
-    lane = lax.broadcasted_iota(jnp.int32, label.shape[1:], 1)
+    tail = (length - 2 * capacity * rows, lanes)
+    lane = lax.broadcasted_iota(jnp.int32, tail, 1)
     for j in range(peers):
-        word = jnp.zeros(label.shape[1:], jnp.int32)
+        word = jnp.zeros(tail, jnp.int32)
         for c in range(capacity):
             word = jnp.where(lane == c, dst_ref[j * capacity + c], word)
-        label[j] = word.astype(f32).astype(bf16)
-    body = 2 * capacity * rows
-    last = pltpu.make_async_copy(
-        label, parcel_ref.at[:, pl.ds(body, length - body)], sems.at[0, 2 * capacity]
-    )
-    last.start()
+        parcel_ref[j, 2 * capacity * rows :, :] = word.astype(f32).astype(bf16)
     for copy in copies:
         copy.wait()
-    last.wait()
 
 
 def pack(keys, values, outgoing, landing, peers):
@@ -401,29 +412,17 @@
         pack_kernel,
         out_shape=jax.ShapeDtypeStruct((peers, 2 * capacity * rows + 16, lanes), bf16),
         in_specs=[SMEM, SMEM, ANY, ANY],
-        out_specs=ANY,
-        scratch_shapes=[
-            pltpu.VMEM((peers, 16, lanes), bf16),
-            pltpu.SemaphoreType.DMA((peers, 2 * capacity + 1)),
-        ],
+        out_specs=VMEM,
+        scratch_shapes=[pltpu.SemaphoreType.DMA((peers, 2 * capacity))],
+        compiler_params=limit(56),
     )(outgoing, landing, keys, values)
 
 
-def place_kernel(src_ref, target_ref, k_ref, v_ref, arrived_ref, mk_ref, mv_ref, blank, sems, page_sems, zero_sems):
-    slots, rows, _ = k_ref.shape
+def place_kernel(src_ref, target_ref, arrived_ref, k_ref, v_ref, mk_ref, mv_ref, blank, page_sems, zero_sems):
+    rows = k_ref.shape[1]
     peers = arrived_ref.shape[0]
     capacity = src_ref.shape[0] // peers
-    parts = sems.shape[1]
-    per = slots // parts
-    copies = []
-    for p in range(parts):
-        for i, (a, b) in enumerate(((k_ref, mk_ref), (v_ref, mv_ref))):
-            part = pl.ds(p * per, per)
-            copies.append(pltpu.make_async_copy(a.at[part], b.at[part], sems.at[i, p]))
-            copies[-1].start()
     blank[...] = jnp.zeros_like(blank)
-    for copy in copies:
-        copy.wait()
 
     def each(act):
         for i, ref in enumerate((mk_ref, mv_ref)):
@@ -446,23 +445,19 @@
 
 
 def place(keys, values, arrived, outgoing, target):
-    slots, rows, lanes = keys.shape
+    rows, lanes = keys.shape[1:]
     peers = arrived.shape[0]
-    capacity = outgoing.shape[0] // peers
-    each = pltpu.SemaphoreType.DMA((2, peers, capacity))
+    each = pltpu.SemaphoreType.DMA((2, peers, outgoing.shape[0] // peers))
     return pl.pallas_call(
         place_kernel,
         out_shape=(jax.ShapeDtypeStruct(keys.shape, bf16),) * 2,
-        in_specs=[SMEM, SMEM, ANY, ANY, ANY],
+        in_specs=[SMEM, SMEM, VMEM, ANY, ANY],
         out_specs=(ANY, ANY),
-        scratch_shapes=[
-            pltpu.VMEM((rows, lanes), bf16),
-            pltpu.SemaphoreType.DMA((2, 8)),
-            each,
-            each,
-        ],
-        cost_estimate=pl.CostEstimate(flops=0, bytes_accessed=2**25, transcendentals=0),
-    )(outgoing, target, keys, values, arrived)
+        input_output_aliases={3: 0, 4: 1},
+        scratch_shapes=[pltpu.VMEM((rows, lanes), bf16), each, each],
+        compiler_params=limit(56),
+        cost_estimate=pl.CostEstimate(flops=0, bytes_accessed=2**21, transcendentals=0),
+    )(outgoing, target, arrived, keys, values)
 
 
 def fresh_kernel(q_ref, nk_ref, nv_ref, mine_ref, out_ref, lse_ref, *, kv_local):
@@ -609,15 +604,16 @@
     values = cache_values.reshape(slots, rows, head_dim)
     outgoing, landing = mig_src.reshape(-1), mig_dst.reshape(-1)
     parcel = pack(keys, values, outgoing, landing, peers)
-    arrived = lax.all_to_all(parcel, "inst", split_axis=0, concat_axis=0, tiled=True)
-    target = arrived[:, 2 * capacity * rows, :capacity].astype(jnp.int32).reshape(-1)
-    moved_keys, moved_values = place(keys, values, arrived, outgoing, target)
-
-    parts = local_attention(keys, values, slot_req, slot_fill, queries, kv_local, peers)
+    parcel, slot_req = lax.optimization_barrier((parcel, slot_req))
+    parts, copied_keys, copied_values = local_attention(keys, values, slot_req, slot_fill, queries, kv_local, peers)
     parts = lax.all_to_all(parts, "inst", split_axis=0, concat_axis=0, tiled=True)
     own = lax.dynamic_slice_in_dim(queries, me * near, near, 0)
     fresh, fresh_lse = fresh_part(own, new_keys, new_values, mine, kv_local)
     blocks = gather_over(combine(parts, fresh, fresh_lse, kv_local), "inst")
+    parcel, _ = lax.optimization_barrier((parcel, blocks[2::2]))
+    arrived = lax.all_to_all(parcel, "inst", split_axis=0, concat_axis=0, tiled=True)
+    target = arrived[:, 2 * capacity * rows, :capacity].astype(jnp.int32).reshape(-1)
+    moved_keys, moved_values = place(copied_keys, copied_values, arrived, outgoing, target)
     shares = project(blocks, out_weight, side, sides)
     lent = lax.ppermute(jnp.stack([shares[1], shares[3]]), "head", mirrored("head", 1))
     kept = shares[0].astype(f32) + lent[0].astype(f32)

time: 418 us -> 129 us (0.31)
  Pallas kernels: 332 us -> 33.2 us
  waiting for transfers between devices: 45 us -> 59.5 us
  local copies, waits for them, and re-layouts: 11.3 us -> 5.48 us
    pallas_call x1, Pallas kernels: 274 us -> 2.61 us  [place(): pl.pallas_call(place_kernel, out_shape=(jax.ShapeDtypeStruct(keys.shape,...]
    all_to_all x1, waiting for transfers between devices: 3.05 us -> 36.6 us  [shards(): lax.all_to_all(parts, 'inst', split_axis=0, concat_axis=0, tiled=True)]
    pallas_call x1, Pallas kernels: 33.9 us -> 3.74 us  [pack(): pl.pallas_call(pack_kernel, out_shape=jax.ShapeDtypeStruct((peers, 2 * ca...]
    ppermute x3, waiting for transfers between devices: 32.6 us -> 9.89 us  [gather_over(): got[k] = lax.ppermute(x, axis, mirrored(axis, k))]
    ppermute x4, waiting for transfers between devices: 7.88 us -> 0.51 us  [gather_over(): got[k + 1] = lax.ppermute(got[k], axis, mirrored(axis, 1))]
    unnamed x22 -> x8, local copies, waits for them, and re-layouts: 7.54 us -> 1.73 us
    all_to_all x1, waiting for transfers between devices: 0.01 us -> 5.49 us  [shards(): lax.all_to_all(parcel, 'inst', split_axis=0, concat_axis=0, tiled=True)]
    ppermute x1, waiting for transfers between devices: 0.01 us -> 5.41 us  [shards(): total = kept + lax.ppermute(passed, 'head', mirrored('head', 2)).astype(f32)]
  transfers between devices with their start and end apart: 11 -> 11, of which waited for: 6 -> 7; matrix products, arithmetic and copies ran while one was open for 1% -> 2% of each run, Pallas kernels for 76% -> 8%
where the time goes in v2:
time: 129 us
  waiting for transfers between devices  59.5 us (46%)
  Pallas kernels  33.2 us (26%)
  starting transfers between devices  28.8 us (22%)
  local copies, waits for them, and re-layouts  5.48 us (4%)
    all_to_all x1, waiting for transfers between devices, shards(): lax.all_to_all(parts, 'inst', split_axis=0, concat_axis=0, tiled=True)  36.6 us
    pallas_call x1, Pallas kernels, local_attention(): pl.pallas_call(attention_kernel, out_shape=(jax.ShapeDtypeStruct((peers,...  15.6 us
    all_to_all x1, starting transfers between devices, shards(): lax.all_to_all(parts, 'inst', split_axis=0, concat_axis=0, tiled=True)  12.5 us
    ppermute x3, waiting for transfers between devices, gather_over(): got[k] = lax.ppermute(x, axis, mirrored(axis, k))  9.89 us
    pallas_call x1, Pallas kernels, project(): pl.pallas_call(functools.partial(project_kernel, sides=sides), out_shape=...  9.27 us
    all_to_all x1, waiting for transfers between devices, shards(): lax.all_to_all(parcel, 'inst', split_axis=0, concat_axis=0, tiled=True)  5.49 us
    ppermute x1, waiting for transfers between devices, shards(): total = kept + lax.ppermute(passed, 'head', mirrored('head', 2)).astype(f32)  5.41 us
    all_to_all x1, starting transfers between devices, shards(): lax.all_to_all(parcel, 'inst', split_axis=0, concat_axis=0, tiled=True)  5.22 us
  transfers between devices with their start and end apart: 11, of which 7 were waited for; matrix products, arithmetic and copies ran while one was open for 2% of the time, Pallas kernels for 8%

profile of v2, /device:TPU:0, one launch (start us, length us, event | category | flops | bytes accessed | tf_op | source)
XLA Modules:
  0.0 128.8 jit_solution(3943826906737572270)
XLA Ops:
  0.6 0.8 copy.18
  2.0 0.8 copy.19
  3.4 3.7 %shard_map.121 = bf16[8,528,128]{2,1,0:T(8,128)(2,1)} custom-call(s32[16]{0:T(128)} %reshape.78.src_ref, s32[16]{0:T(128)} %reshape.79.dst_ref, bf16[128,128,128]{2,1,0:T(8,128)(2,1)} %bitcast.19, bf16[128,128,128]{2,1,0:T(8,128)(2,1)} %bitcast.21), custom_call_target="tpu_custom_call" | custom-call | tf_op jit(solution)/shard_map/pallas_call | solution.py:411
  7.2 15.6 %shard_map.122 = (bf16[8,800,128]{2,1,0:T(8,128)(2,1)}, bf16[128,128,128]{2,1,0:T(8,128)(2,1)}, bf16[128,128,128]{2,1,0:T(8,128)(2,1)}) custom-call(s32[128]{0:T(128)} %req_ref, s32[128]{0:T(128)} %fill_ref.1, bf16[16,12,32,128]{3,2,1,0:T(8,128)(2,1)} %q_ref.1, bf16[128,128,128]{2,1,0:T(8,128)(2,1)} %bitcast.20, bf16[128,128,128]{2,1,0:T(8,128)(2,1)} %bitcast.22), custom_call_target="tpu_custom_call" | custom-call | flops 3000000000 | bytes 16777216 | tf_op jit(solution)/shard_map/pallas_call | solution.py:347
  22.8 12.5 %all-to-all-start = ((bf16[8,800,128]{2,1,0:T(8,128)(2,1)}), bf16[8,800,128]{2,1,0:T(8,128)(2,1)S(1)}, u32[]{:S(2)}, u32[]{:S(2)}) async-start(bf16[8,800,128]{2,1,0:T(8,128)(2,1)} %get-tuple-element.15), calls=%async_computation | async-start | bytes 3276800 | tf_op jit(solution)/shard_map/all_to_all | solution.py:609
  35.4 0.9 constant_dynamic-slice_fusion.q_ref
  37.1 36.6 %all-to-all-done.parts_ref = bf16[8,800,128]{2,1,0:T(8,128)(2,1)S(1)} async-done(((bf16[8,800,128]{2,1,0:T(8,128)(2,1)}), bf16[8,800,128]{2,1,0:T(8,128)(2,1)S(1)}, u32[]{:S(2)}, u32[]{:S(2)}) %all-to-all-start) | async-done | bytes 1638432 | tf_op jit(solution)/shard_map/all_to_all | solution.py:609
  73.7 1.2 shard_map.124.refs_0_
  75.0 2.7 %collective-permute-start.1 = (bf16[24,4096]{1,0:T(8,128)(2,1)S(1)}, bf16[24,4096]{1,0:T(8,128)(2,1)S(1)}, u32[]{:S(2)}, u32[]{:S(2)}) collective-permute-start(bf16[24,4096]{1,0:T(8,128)(2,1)S(1)} %shard_map.124.refs_0_), channel_id=1, source_target_pairs={{0,16},{4,20},{8,24},{12,28},{16,0},{20,4},{24,8},{28,12},{1,17},{... | collective-permute-start | bytes 589832 | tf_op jit(solution)/shard_map/ppermute | solution.py:583
  77.7 1.7 %collective-permute-start.2 = (bf16[24,4096]{1,0:T(8,128)(2,1)S(1)}, bf16[24,4096]{1,0:T(8,128)(2,1)S(1)}, u32[]{:S(2)}, u32[]{:S(2)}) collective-permute-start(bf16[24,4096]{1,0:T(8,128)(2,1)S(1)} %shard_map.124.refs_0_), channel_id=1, source_target_pairs={{0,24},{4,28},{8,16},{12,20},{16,8},{20,12},{24,0},{28,4},{1,25},{... | collective-permute-start | bytes 589832 | tf_op jit(solution)/shard_map/ppermute | solution.py:583
  79.4 1.5 %collective-permute-start.3 = (bf16[24,4096]{1,0:T(8,128)(2,1)S(1)}, bf16[24,4096]{1,0:T(8,128)(2,1)S(1)}, u32[]{:S(2)}, u32[]{:S(2)}) collective-permute-start(bf16[24,4096]{1,0:T(8,128)(2,1)S(1)} %shard_map.124.refs_0_), channel_id=1, source_target_pairs={{0,4},{4,0},{8,12},{12,8},{16,20},{20,16},{24,28},{28,24},{1,5},{5... | collective-permute-start | bytes 589832 | tf_op jit(solution)/shard_map/ppermute | solution.py:585
  80.9 3.1 %collective-permute-done.refs_2_ = bf16[24,4096]{1,0:T(8,128)(2,1)S(1)} collective-permute-done((bf16[24,4096]{1,0:T(8,128)(2,1)S(1)}, bf16[24,4096]{1,0:T(8,128)(2,1)S(1)}, u32[]{:S(2)}, u32[]{:S(2)}) %collective-permute-start) | collective-permute-done | bytes 196640 | tf_op jit(solution)/shard_map/ppermute | solution.py:583
  84.0 1.5 %collective-permute-start.4 = (bf16[24,4096]{1,0:T(8,128)(2,1)S(1)}, bf16[24,4096]{1,0:T(8,128)(2,1)S(1)}, u32[]{:S(2)}, u32[]{:S(2)}) collective-permute-start(bf16[24,4096]{1,0:T(8,128)(2,1)S(1)} %collective-permute-done.refs_2_), channel_id=1, source_target_pairs={{0,4},{4,0},{8,12},{12,8},{16,20},{20,16},{24,28},{28,24},{1,5},{5... | collective-permute-start | bytes 589832 | tf_op jit(solution)/shard_map/ppermute | solution.py:585
  85.5 6.8 %collective-permute-done.1.refs_4_ = bf16[24,4096]{1,0:T(8,128)(2,1)S(1)} collective-permute-done((bf16[24,4096]{1,0:T(8,128)(2,1)S(1)}, bf16[24,4096]{1,0:T(8,128)(2,1)S(1)}, u32[]{:S(2)}, u32[]{:S(2)}) %collective-permute-start.1) | collective-permute-done | bytes 196640 | tf_op jit(solution)/shard_map/ppermute | solution.py:583
  92.2 1.5 %collective-permute-start.5 = (bf16[24,4096]{1,0:T(8,128)(2,1)S(1)}, bf16[24,4096]{1,0:T(8,128)(2,1)S(1)}, u32[]{:S(2)}, u32[]{:S(2)}) collective-permute-start(bf16[24,4096]{1,0:T(8,128)(2,1)S(1)} %collective-permute-done.1.refs_4_), channel_id=1, source_target_pairs={{0,4},{4,0},{8,12},{12,8},{16,20},{20,16},{24,28},{28,24},{1,5},{5... | collective-permute-start | bytes 589832 | tf_op jit(solution)/shard_map/ppermute | solution.py:585
  94.3 5.2 %all-to-all-start.1 = ((bf16[8,528,128]{2,1,0:T(8,128)(2,1)}), bf16[8,528,128]{2,1,0:T(8,128)(2,1)S(1)}, u32[]{:S(2)}, u32[]{:S(2)}) async-start(bf16[8,528,128]{2,1,0:T(8,128)(2,1)} %shard_map.121), calls=%async_computation.1 | async-start | bytes 2162688 | tf_op jit(solution)/shard_map/all_to_all | solution.py:614
  100.0 9.3 %shard_map.126 = bf16[4,192,512]{2,1,0:T(8,128)(2,1)S(1)} custom-call(s32[1]{0:T(128)} %bitcast.7.mine_ref, bf16[24,4096]{1,0:T(8,128)(2,1)S(1)} %shard_map.124.refs_0_, bf16[24,4096]{1,0:T(8,128)(2,1)S(1)} %collective-permute-done.3.refs_1_, bf16[24,4096]{1,0:T(8,128)(2,1)S(1)} %collective-permute-done.refs_2_, ...), custom_call_target="tpu_custom_call" | custom-call | tf_op jit(solution)/shard_map/pallas_call | solution.py:565
  109.6 1.5 %collective-permute-done.7 = bf16[2,192,512]{2,1,0:T(8,128)(2,1)S(1)} collective-permute-done((bf16[2,192,512]{2,1,0:T(8,128)(2,1)S(1)}, bf16[2,192,512]{2,1,0:T(8,128)(2,1)S(1)}, u32[]{:S(2)}, u32[]{:S(2)}) %collective-permute-start.7) | collective-permute-done | bytes 393248 | tf_op jit(solution)/shard_map/ppermute | solution.py:618
  111.2 1.6 %collective-permute-start.8 = (bf16[192,512]{1,0:T(8,128)(2,1)S(1)}, bf16[192,512]{1,0:T(8,128)(2,1)S(1)}, u32[]{:S(2)}, u32[]{:S(2)}) collective-permute-start(bf16[192,512]{1,0:T(8,128)(2,1)S(1)} %fusion.1), channel_id=1, source_target_pairs={{0,2},{1,3},{2,0},{3,1},{4,6},{5,7},{6,4},{7,5},{8,10},{9,11},{10,... | collective-permute-start | bytes 589832 | tf_op jit(solution)/shard_map/ppermute | solution.py:621
  112.8 5.4 %collective-permute-done.8 = bf16[192,512]{1,0:T(8,128)(2,1)S(1)} collective-permute-done((bf16[192,512]{1,0:T(8,128)(2,1)S(1)}, bf16[192,512]{1,0:T(8,128)(2,1)S(1)}, u32[]{:S(2)}, u32[]{:S(2)}) %collective-permute-start.8) | collective-permute-done | bytes 196640 | tf_op jit(solution)/shard_map/ppermute | solution.py:621
  118.9 0.8 copy_select_fusion
  119.7 5.5 %all-to-all-done.1.arrived_ref = bf16[8,528,128]{2,1,0:T(8,128)(2,1)S(1)} async-done(((bf16[8,528,128]{2,1,0:T(8,128)(2,1)}), bf16[8,528,128]{2,1,0:T(8,128)(2,1)S(1)}, u32[]{:S(2)}, u32[]{:S(2)}) %all-to-all-start.1) | async-done | bytes 1081376 | tf_op jit(solution)/shard_map/all_to_all | solution.py:614
  125.2 0.8 reshape.95.target_ref
  126.2 2.6 %shard_map.125 = (bf16[128,128,128]{2,1,0:T(8,128)(2,1)}, bf16[128,128,128]{2,1,0:T(8,128)(2,1)}) custom-call(s32[16]{0:T(128)} %reshape.78.src_ref, s32[16]{0:T(128)} %reshape.95.target_ref, bf16[8,528,128]{2,1,0:T(8,128)(2,1)} %copy-done, bf16[128,128,128]{2,1,0:T(8,128)(2,1)} %get-tuple-element.19.k_ref, ...), custom_call_target="tpu_custom_call", output_to_operand_aliasing={{0}: (3, {}), {1}: (4, {})} | custom-call | bytes 2097152 | tf_op jit(solution)/shard_map/pallas_call | solution.py:451
  (31 shorter events, 4.4 us)
Async XLA Ops:
  7.1 28.2 %copy-start.1 = (bf16[16,12,2,128]{3,2,1,0:T(2,128)(2,1)S(1)}, bf16[16,12,2,128]{3,2,1,0:T(2,128)(2,1)}, u32[]{:S(2)}) copy-start(bf16[16,12,2,128]{3,2,1,0:T(2,128)(2,1)} %param.17) | copy-start | bytes 294916
  7.1 28.2 %copy-start.2 = (bf16[16,12,2,128]{3,2,1,0:T(2,128)(2,1)S(1)}, bf16[16,12,2,128]{3,2,1,0:T(2,128)(2,1)}, u32[]{:S(2)}) copy-start(bf16[16,12,2,128]{3,2,1,0:T(2,128)(2,1)} %param.18) | copy-start | bytes 294916
  22.8 50.9 %all-to-all-start = ((bf16[8,800,128]{2,1,0:T(8,128)(2,1)}), bf16[8,800,128]{2,1,0:T(8,128)(2,1)S(1)}, u32[]{:S(2)}, u32[]{:S(2)}) async-start(bf16[8,800,128]{2,1,0:T(8,128)(2,1)} %get-tuple-element.15), calls=%async_computation | async-start | bytes 3276800 | tf_op jit(solution)/shard_map/all_to_all | solution.py:609
  75.0 9.0 %collective-permute-start = (bf16[24,4096]{1,0:T(8,128)(2,1)S(1)}, bf16[24,4096]{1,0:T(8,128)(2,1)S(1)}, u32[]{:S(2)}, u32[]{:S(2)}) collective-permute-start(bf16[24,4096]{1,0:T(8,128)(2,1)S(1)} %shard_map.124.refs_0_), channel_id=1, source_target_pairs={{0,8},{4,12},{8,0},{12,4},{16,24},{20,28},{24,16},{28,20},{1,9},{5... | collective-permute-start | bytes 589832 | tf_op jit(solution)/shard_map/ppermute | solution.py:583
  75.0 17.2 %collective-permute-start.1 = (bf16[24,4096]{1,0:T(8,128)(2,1)S(1)}, bf16[24,4096]{1,0:T(8,128)(2,1)S(1)}, u32[]{:S(2)}, u32[]{:S(2)}) collective-permute-start(bf16[24,4096]{1,0:T(8,128)(2,1)S(1)} %shard_map.124.refs_0_), channel_id=1, source_target_pairs={{0,16},{4,20},{8,24},{12,28},{16,0},{20,4},{24,8},{28,12},{1,17},{... | collective-permute-start | bytes 589832 | tf_op jit(solution)/shard_map/ppermute | solution.py:583
  77.7 16.0 %collective-permute-start.2 = (bf16[24,4096]{1,0:T(8,128)(2,1)S(1)}, bf16[24,4096]{1,0:T(8,128)(2,1)S(1)}, u32[]{:S(2)}, u32[]{:S(2)}) collective-permute-start(bf16[24,4096]{1,0:T(8,128)(2,1)S(1)} %shard_map.124.refs_0_), channel_id=1, source_target_pairs={{0,24},{4,28},{8,16},{12,20},{16,8},{20,12},{24,0},{28,4},{1,25},{... | collective-permute-start | bytes 589832 | tf_op jit(solution)/shard_map/ppermute | solution.py:583
  79.4 20.1 %collective-permute-start.3 = (bf16[24,4096]{1,0:T(8,128)(2,1)S(1)}, bf16[24,4096]{1,0:T(8,128)(2,1)S(1)}, u32[]{:S(2)}, u32[]{:S(2)}) collective-permute-start(bf16[24,4096]{1,0:T(8,128)(2,1)S(1)} %shard_map.124.refs_0_), channel_id=1, source_target_pairs={{0,4},{4,0},{8,12},{12,8},{16,20},{20,16},{24,28},{28,24},{1,5},{5... | collective-permute-start | bytes 589832 | tf_op jit(solution)/shard_map/ppermute | solution.py:585
  84.0 15.5 %collective-permute-start.4 = (bf16[24,4096]{1,0:T(8,128)(2,1)S(1)}, bf16[24,4096]{1,0:T(8,128)(2,1)S(1)}, u32[]{:S(2)}, u32[]{:S(2)}) collective-permute-start(bf16[24,4096]{1,0:T(8,128)(2,1)S(1)} %collective-permute-done.refs_2_), channel_id=1, source_target_pairs={{0,4},{4,0},{8,12},{12,8},{16,20},{20,16},{24,28},{28,24},{1,5},{5... | collective-permute-start | bytes 589832 | tf_op jit(solution)/shard_map/ppermute | solution.py:585
  92.2 7.3 %collective-permute-start.5 = (bf16[24,4096]{1,0:T(8,128)(2,1)S(1)}, bf16[24,4096]{1,0:T(8,128)(2,1)S(1)}, u32[]{:S(2)}, u32[]{:S(2)}) collective-permute-start(bf16[24,4096]{1,0:T(8,128)(2,1)S(1)} %collective-permute-done.1.refs_4_), channel_id=1, source_target_pairs={{0,4},{4,0},{8,12},{12,8},{16,20},{20,16},{24,28},{28,24},{1,5},{5... | collective-permute-start | bytes 589832 | tf_op jit(solution)/shard_map/ppermute | solution.py:585
  93.7 6.3 %collective-permute-start.6 = (bf16[24,4096]{1,0:T(8,128)(2,1)S(1)}, bf16[24,4096]{1,0:T(8,128)(2,1)S(1)}, u32[]{:S(2)}, u32[]{:S(2)}) collective-permute-start(bf16[24,4096]{1,0:T(8,128)(2,1)S(1)} %collective-permute-done.2.refs_6_), channel_id=1, source_target_pairs={{0,4},{4,0},{8,12},{12,8},{16,20},{20,16},{24,28},{28,24},{1,5},{5... | collective-permute-start | bytes 589832 | tf_op jit(solution)/shard_map/ppermute | solution.py:585
  94.3 31.0 %all-to-all-start.1 = ((bf16[8,528,128]{2,1,0:T(8,128)(2,1)}), bf16[8,528,128]{2,1,0:T(8,128)(2,1)S(1)}, u32[]{:S(2)}, u32[]{:S(2)}) async-start(bf16[8,528,128]{2,1,0:T(8,128)(2,1)} %shard_map.121), calls=%async_computation.1 | async-start | bytes 2162688 | tf_op jit(solution)/shard_map/all_to_all | solution.py:614
  109.4 1.8 %collective-permute-start.7 = (bf16[2,192,512]{2,1,0:T(8,128)(2,1)S(1)}, bf16[2,192,512]{2,1,0:T(8,128)(2,1)S(1)}, u32[]{:S(2)}, u32[]{:S(2)}) collective-permute-start(bf16[2,192,512]{2,1,0:T(8,128)(2,1)S(1)} %pad_maximum_fusion), channel_id=1, source_target_pairs={{0,1},{1,0},{2,3},{3,2},{4,5},{5,4},{6,7},{7,6},{8,9},{9,8},{10,11... | collective-permute-start | bytes 1179656 | tf_op jit(solution)/shard_map/ppermute | solution.py:618
  111.2 7.0 %collective-permute-start.8 = (bf16[192,512]{1,0:T(8,128)(2,1)S(1)}, bf16[192,512]{1,0:T(8,128)(2,1)S(1)}, u32[]{:S(2)}, u32[]{:S(2)}) collective-permute-start(bf16[192,512]{1,0:T(8,128)(2,1)S(1)} %fusion.1), channel_id=1, source_target_pairs={{0,2},{1,3},{2,0},{3,1},{4,6},{5,7},{6,4},{7,5},{8,10},{9,11},{10,... | collective-permute-start | bytes 589832 | tf_op jit(solution)/shard_map/ppermute | solution.py:621
  125.2 1.0 copy-start

commit v3 on v2

--- a/solution.py
+++ b/solution.py
@@ -460,7 +460,9 @@
     )(outgoing, target, arrived, keys, values)
 
 
-def fresh_kernel(q_ref, nk_ref, nv_ref, mine_ref, out_ref, lse_ref, *, kv_local):
+def fresh_kernel(q_ref, nk_ref, nv_ref, mine_ref, out_ref, lse_ref, nk_wide, nv_wide, *, kv_local):
+    nk_wide[...] = nk_ref[...].astype(f32)
+    nv_wide[...] = nv_ref[...].astype(f32)
     near, requests, heads, head_dim = q_ref.shape
     steps = nk_ref.shape[0]
     group = heads // kv_local
@@ -474,12 +476,12 @@
         for k in range(kv_local):
             n = r * kv_local + k
             q = q_ref[:, r, k * group : (k + 1) * group, :].reshape(rows, head_dim)
-            s = lax.dot_general(q, nk_ref[:, n, :].astype(bf16), (((1,), (1,)), ((), ())), preferred_element_type=f32)
+            s = lax.dot_general(q, nk_wide[:, n, :].astype(bf16), (((1,), (1,)), ((), ())), preferred_element_type=f32)
             s = jnp.where(live, s * scale, masked_score)
             m = s.max(axis=1, keepdims=True)
             p = jnp.exp2(s - m)
             l = p.sum(axis=1, keepdims=True)
-            o = jnp.dot(p.astype(bf16), nv_ref[:, n, :].astype(bf16), preferred_element_type=f32) * (1.0 / l)
+            o = jnp.dot(p.astype(bf16), nv_wide[:, n, :].astype(bf16), preferred_element_type=f32) * (1.0 / l)
             out_ref[:, r, k * group : (k + 1) * group, :] = o.reshape(near, group, head_dim)
             lse = jnp.where(lane == n, m + jnp.log2(l), lse)
     lse_ref[...] = lse
@@ -497,9 +499,10 @@
         ),
         in_specs=[VMEM, VMEM, VMEM, SMEM],
         out_specs=(VMEM, VMEM),
+        scratch_shapes=[pltpu.VMEM(wide, f32)] * 2,
         compiler_params=limit(16),
         cost_estimate=pl.CostEstimate(flops=10**8, bytes_accessed=2**21, transcendentals=10**5),
-    )(queries, new_keys.astype(f32).reshape(wide), new_values.astype(f32).reshape(wide), mine)
+    )(queries, new_keys.reshape(wide), new_values.reshape(wide), mine)
 
 
 def combine_kernel(parts_ref, fresh_ref, fresh_lse_ref, out_ref, rows_ref, *, kv_local):
@@ -545,15 +548,24 @@
     )(parts, fresh, fresh_lse)
 
 
-def project_kernel(mine_ref, *refs, sides):
-    blocks, (w_ref, out_ref, rows_ref, sums_ref) = refs[:-4], refs[-4:]
+def project_kernel(mine_ref, w_ref, *refs, sides):
+    blocks, (out_ref, rows_ref, x_ref, panels, sums_ref, sems) = refs[:-6], refs[-6:]
+    parts = sems.shape[0]
+    deep = w_ref.shape[0] // parts
+    copies = [pltpu.make_async_copy(w_ref.at[pl.ds(a * deep, deep)], panels.at[a], sems.at[a]) for a in range(parts)]
+    for copy in copies:
+        copy.start()
     rows = blocks[0].shape[0]
     for i, block in enumerate(blocks):
         rows_ref[i * rows : (i + 1) * rows, :] = block[...].astype(f32)
+    x_ref[...] = rows_ref[...].astype(bf16)
     width = w_ref.shape[1] // sides
-    x = rows_ref[...].astype(bf16)
-    for b in range(sides):
-        sums_ref[b] = jnp.dot(x, w_ref[:, b * width : (b + 1) * width], preferred_element_type=f32)
+    for a, copy in enumerate(copies):
+        copy.wait()
+        x = x_ref[:, a * deep : (a + 1) * deep]
+        for b in range(sides):
+            y = jnp.dot(x, panels[a, :, b * width : (b + 1) * width], preferred_element_type=f32)
+            sums_ref[b] = y if a == 0 else sums_ref[b] + y
     for p in range(sides):
         out_ref[p] = sums_ref[p ^ mine_ref[0]].astype(bf16)
 
@@ -562,14 +574,21 @@
     rows, depth = blocks[0].shape
     rows *= len(blocks)
     width = weight.shape[1] // sides
+    parts = 8
     return pl.pallas_call(
         functools.partial(project_kernel, sides=sides),
         out_shape=jax.ShapeDtypeStruct((sides, rows, width), bf16),
-        in_specs=[SMEM] + [VMEM] * (len(blocks) + 1),
+        in_specs=[SMEM, ANY] + [VMEM] * len(blocks),
         out_specs=VMEM,
-        scratch_shapes=[pltpu.VMEM((rows, depth), f32), pltpu.VMEM((sides, rows, width), f32)],
-        compiler_params=limit(40),
-    )(mine, *blocks, weight)
+        scratch_shapes=[
+            pltpu.VMEM((rows, depth), f32),
+            pltpu.VMEM((rows, depth), bf16),
+            pltpu.VMEM((parts, depth // parts, weight.shape[1]), bf16),
+            pltpu.VMEM((sides, rows, width), f32),
+            pltpu.SemaphoreType.DMA((parts,)),
+        ],
+        compiler_params=limit(54),
+    )(mine, weight, *blocks)
 
 
 def mirrored(axis, k):
@@ -604,11 +623,11 @@
     values = cache_values.reshape(slots, rows, head_dim)
     outgoing, landing = mig_src.reshape(-1), mig_dst.reshape(-1)
     parcel = pack(keys, values, outgoing, landing, peers)
-    parcel, slot_req = lax.optimization_barrier((parcel, slot_req))
     parts, copied_keys, copied_values = local_attention(keys, values, slot_req, slot_fill, queries, kv_local, peers)
     parts = lax.all_to_all(parts, "inst", split_axis=0, concat_axis=0, tiled=True)
     own = lax.dynamic_slice_in_dim(queries, me * near, near, 0)
     fresh, fresh_lse = fresh_part(own, new_keys, new_values, mine, kv_local)
+    parcel, fresh_lse = lax.optimization_barrier((parcel, fresh_lse))
     blocks = gather_over(combine(parts, fresh, fresh_lse, kv_local), "inst")
     parcel, _ = lax.optimization_barrier((parcel, blocks[2::2]))
     arrived = lax.all_to_all(parcel, "inst", split_axis=0, concat_axis=0, tiled=True)

time: 129 us -> 122 us (0.946)
  waiting for transfers between devices: 59.5 us -> 51.3 us
  starting transfers between devices: 28.8 us -> 22.3 us
  Pallas kernels: 33.2 us -> 38.2 us
  other arithmetic: 1.04 us -> 2.86 us
    all_to_all x1, starting transfers between devices: 12.5 us -> 6.04 us  [shards(): lax.all_to_all(parts, 'inst', split_axis=0, concat_axis=0, tiled=True)]
    pallas_call x1, Pallas kernels: 15.6 us -> 21.1 us  [local_attention(): pl.pallas_call(attention_kernel, out_shape=(jax.ShapeDtypeStruct((peers,...]
    all_to_all x1, waiting for transfers between devices: 36.6 us -> 31.7 us  [shards(): lax.all_to_all(parts, 'inst', split_axis=0, concat_axis=0, tiled=True)]
    all_to_all x1, waiting for transfers between devices: 5.49 us -> 2.3 us  [shards(): lax.all_to_all(parcel, 'inst', split_axis=0, concat_axis=0, tiled=True)]
  transfers between devices with their start and end apart: 11 -> 11, of which waited for: 7 -> 7; matrix products, arithmetic and copies ran while one was open for 2% -> 6% of each run, Pallas kernels for 8% -> 11%
where the time goes in v3:
time: 122 us; the launch traced here: 121 us
  waiting for transfers between devices  51.3 us (42%)
  Pallas kernels  38.2 us (31%)
  starting transfers between devices  22.3 us (18%)
  local copies, waits for them, and re-layouts  5.86 us (5%)
  other arithmetic  2.86 us (2%)
    all_to_all x1, waiting for transfers between devices, shards(): lax.all_to_all(parts, 'inst', split_axis=0, concat_axis=0, tiled=True)  31.7 us
    pallas_call x1, Pallas kernels, local_attention(): pl.pallas_call(attention_kernel, out_shape=(jax.ShapeDtypeStruct((peers,...  21.1 us
    ppermute x3, waiting for transfers between devices, gather_over(): got[k] = lax.ppermute(x, axis, mirrored(axis, k))  9.88 us
    pallas_call x1, Pallas kernels, project(): pl.pallas_call(functools.partial(project_kernel, sides=sides), out_shape=...  8.93 us
    all_to_all x1, starting transfers between devices, shards(): lax.all_to_all(parts, 'inst', split_axis=0, concat_axis=0, tiled=True)  6.04 us
    ppermute x1, waiting for transfers between devices, shards(): total = kept + lax.ppermute(passed, 'head', mirrored('head', 2)).astype(f32)  5.41 us
    all_to_all x1, starting transfers between devices, shards(): lax.all_to_all(parcel, 'inst', split_axis=0, concat_axis=0, tiled=True)  5.21 us
    ppermute x4, starting transfers between devices, gather_over(): got[k + 1] = lax.ppermute(got[k], axis, mirrored(axis, 1))  4.97 us
  transfers between devices with their start and end apart: 11, of which 7 were waited for; matrix products, arithmetic and copies ran while one was open for 6% of the time, Pallas kernels for 11%

profile of v3, /device:TPU:0, one launch (start us, length us, event | category | flops | bytes accessed | tf_op | source)
XLA Modules:
  0.0 121.4 jit_solution(5913314406287504914)
XLA Ops:
  0.7 21.1 %shard_map.123 = (bf16[8,800,128]{2,1,0:T(8,128)(2,1)}, bf16[128,128,128]{2,1,0:T(8,128)(2,1)}, bf16[128,128,128]{2,1,0:T(8,128)(2,1)}) custom-call(s32[128]{0:T(128)} %req_ref.1, s32[128]{0:T(128)} %fill_ref.1, bf16[16,12,32,128]{3,2,1,0:T(8,128)(2,1)} %q_ref.1, bf16[128,128,128]{2,1,0:T(8,128)(2,1)} %bitcast.19, bf16[128,128,128]{2,1,0:T(8,128)(2,1)} %bitcast.21), custom_call_target="tpu_custom_call" | custom-call | flops 3000000000 | bytes 16777216 | tf_op jit(solution)/shard_map/pallas_call | solution.py:347
  21.8 6.0 %all-to-all-start = ((bf16[8,800,128]{2,1,0:T(8,128)(2,1)}), bf16[8,800,128]{2,1,0:T(8,128)(2,1)S(1)}, u32[]{:S(2)}, u32[]{:S(2)}) async-start(bf16[8,800,128]{2,1,0:T(8,128)(2,1)} %get-tuple-element.15), calls=%async_computation | async-start | bytes 3276800 | tf_op jit(solution)/shard_map/all_to_all | solution.py:627
  29.3 3.5 %shard_map.121 = bf16[8,528,128]{2,1,0:T(8,128)(2,1)} custom-call(s32[16]{0:T(128)} %reshape.74.src_ref, s32[16]{0:T(128)} %reshape.75.dst_ref, bf16[128,128,128]{2,1,0:T(8,128)(2,1)} %bitcast.20, bf16[128,128,128]{2,1,0:T(8,128)(2,1)} %bitcast.22), custom_call_target="tpu_custom_call" | custom-call | tf_op jit(solution)/shard_map/pallas_call | solution.py:411
  32.8 0.9 constant_dynamic-slice_fusion.q_ref
  34.5 31.7 %all-to-all-done.parts_ref = bf16[8,800,128]{2,1,0:T(8,128)(2,1)S(1)} async-done(((bf16[8,800,128]{2,1,0:T(8,128)(2,1)}), bf16[8,800,128]{2,1,0:T(8,128)(2,1)S(1)}, u32[]{:S(2)}, u32[]{:S(2)}) %all-to-all-start) | async-done | bytes 1638432 | tf_op jit(solution)/shard_map/all_to_all | solution.py:627
  66.3 1.2 %shard_map.124.refs_0_ = bf16[24,4096]{1,0:T(8,128)(2,1)S(1)} custom-call(bf16[8,800,128]{2,1,0:T(8,128)(2,1)S(1)} %all-to-all-done.parts_ref, f32[2,12,32,128]{3,2,1,0:T(8,128)S(1)} %get-tuple-element.16.fresh_ref, f32[32,128]{1,0:T(8,128)S(1)} %get-tuple-element.17.fresh_lse_ref), custom_call_target="tpu_custom_call" | custom-call | tf_op jit(solution)/shard_map/pallas_call | solution.py:541
  67.6 2.7 %collective-permute-start.1 = (bf16[24,4096]{1,0:T(8,128)(2,1)S(1)}, bf16[24,4096]{1,0:T(8,128)(2,1)S(1)}, u32[]{:S(2)}, u32[]{:S(2)}) collective-permute-start(bf16[24,4096]{1,0:T(8,128)(2,1)S(1)} %shard_map.124.refs_0_), channel_id=1, source_target_pairs={{0,16},{4,20},{8,24},{12,28},{16,0},{20,4},{24,8},{28,12},{1,17},{... | collective-permute-start | bytes 589832 | tf_op jit(solution)/shard_map/ppermute | solution.py:602
  70.3 1.7 %collective-permute-start.2 = (bf16[24,4096]{1,0:T(8,128)(2,1)S(1)}, bf16[24,4096]{1,0:T(8,128)(2,1)S(1)}, u32[]{:S(2)}, u32[]{:S(2)}) collective-permute-start(bf16[24,4096]{1,0:T(8,128)(2,1)S(1)} %shard_map.124.refs_0_), channel_id=1, source_target_pairs={{0,24},{4,28},{8,16},{12,20},{16,8},{20,12},{24,0},{28,4},{1,25},{... | collective-permute-start | bytes 589832 | tf_op jit(solution)/shard_map/ppermute | solution.py:602
  72.0 1.5 %collective-permute-start.3 = (bf16[24,4096]{1,0:T(8,128)(2,1)S(1)}, bf16[24,4096]{1,0:T(8,128)(2,1)S(1)}, u32[]{:S(2)}, u32[]{:S(2)}) collective-permute-start(bf16[24,4096]{1,0:T(8,128)(2,1)S(1)} %shard_map.124.refs_0_), channel_id=1, source_target_pairs={{0,4},{4,0},{8,12},{12,8},{16,20},{20,16},{24,28},{28,24},{1,5},{5... | collective-permute-start | bytes 589832 | tf_op jit(solution)/shard_map/ppermute | solution.py:604
  73.4 3.1 %collective-permute-done.refs_2_ = bf16[24,4096]{1,0:T(8,128)(2,1)S(1)} collective-permute-done((bf16[24,4096]{1,0:T(8,128)(2,1)S(1)}, bf16[24,4096]{1,0:T(8,128)(2,1)S(1)}, u32[]{:S(2)}, u32[]{:S(2)}) %collective-permute-start) | collective-permute-done | bytes 196640 | tf_op jit(solution)/shard_map/ppermute | solution.py:602
  76.6 1.5 %collective-permute-start.4 = (bf16[24,4096]{1,0:T(8,128)(2,1)S(1)}, bf16[24,4096]{1,0:T(8,128)(2,1)S(1)}, u32[]{:S(2)}, u32[]{:S(2)}) collective-permute-start(bf16[24,4096]{1,0:T(8,128)(2,1)S(1)} %collective-permute-done.refs_2_), channel_id=1, source_target_pairs={{0,4},{4,0},{8,12},{12,8},{16,20},{20,16},{24,28},{28,24},{1,5},{5... | collective-permute-start | bytes 589832 | tf_op jit(solution)/shard_map/ppermute | solution.py:604
  78.0 6.8 %collective-permute-done.1.refs_4_ = bf16[24,4096]{1,0:T(8,128)(2,1)S(1)} collective-permute-done((bf16[24,4096]{1,0:T(8,128)(2,1)S(1)}, bf16[24,4096]{1,0:T(8,128)(2,1)S(1)}, u32[]{:S(2)}, u32[]{:S(2)}) %collective-permute-start.1) | collective-permute-done | bytes 196640 | tf_op jit(solution)/shard_map/ppermute | solution.py:602
  84.8 1.5 %collective-permute-start.5 = (bf16[24,4096]{1,0:T(8,128)(2,1)S(1)}, bf16[24,4096]{1,0:T(8,128)(2,1)S(1)}, u32[]{:S(2)}, u32[]{:S(2)}) collective-permute-start(bf16[24,4096]{1,0:T(8,128)(2,1)S(1)} %collective-permute-done.1.refs_4_), channel_id=1, source_target_pairs={{0,4},{4,0},{8,12},{12,8},{16,20},{20,16},{24,28},{28,24},{1,5},{5... | collective-permute-start | bytes 589832 | tf_op jit(solution)/shard_map/ppermute | solution.py:604
  86.8 5.2 %all-to-all-start.1 = ((bf16[8,528,128]{2,1,0:T(8,128)(2,1)}), bf16[8,528,128]{2,1,0:T(8,128)(2,1)S(1)}, u32[]{:S(2)}, u32[]{:S(2)}) async-start(bf16[8,528,128]{2,1,0:T(8,128)(2,1)} %shard_map.121), calls=%async_computation.1 | async-start | bytes 2162688 | tf_op jit(solution)/shard_map/all_to_all | solution.py:633
  93.2 8.9 %shard_map.126 = bf16[4,192,512]{2,1,0:T(8,128)(2,1)} custom-call(s32[1]{0:T(128)} %bitcast.7.mine_ref, bf16[4096,2048]{1,0:T(8,128)(2,1)} %w_ref.1, bf16[24,4096]{1,0:T(8,128)(2,1)} %copy-done, bf16[24,4096]{1,0:T(8,128)(2,1)} %copy-done.7, bf16[24,4096]{1,0:T(8,128)(2,1)} %copy-done.4, bf16[24,4096]{1,0:T(8,128)(2,1)} %copy-done.8, ...), custom_call_target="tpu_custom_call" | custom-call | tf_op jit(solution)/shard_map/pallas_call | solution.py:578
  102.2 1.0 fusion.4
  103.5 1.5 %collective-permute-done.7 = bf16[2,192,512]{2,1,0:T(8,128)(2,1)S(1)} collective-permute-done((bf16[2,192,512]{2,1,0:T(8,128)(2,1)S(1)}, bf16[2,192,512]{2,1,0:T(8,128)(2,1)S(1)}, u32[]{:S(2)}, u32[]{:S(2)}) %collective-permute-start.7) | collective-permute-done | bytes 393248 | tf_op jit(solution)/shard_map/ppermute | solution.py:637
  105.1 1.0 fusion.1
  106.0 1.6 %collective-permute-start.8 = (bf16[192,512]{1,0:T(8,128)(2,1)S(1)}, bf16[192,512]{1,0:T(8,128)(2,1)S(1)}, u32[]{:S(2)}, u32[]{:S(2)}) collective-permute-start(bf16[192,512]{1,0:T(8,128)(2,1)S(1)} %fusion.1), channel_id=1, source_target_pairs={{0,2},{1,3},{2,0},{3,1},{4,6},{5,7},{6,4},{7,5},{8,10},{9,11},{10,... | collective-permute-start | bytes 589832 | tf_op jit(solution)/shard_map/ppermute | solution.py:640
  107.6 5.4 %collective-permute-done.8 = bf16[192,512]{1,0:T(8,128)(2,1)S(1)} collective-permute-done((bf16[192,512]{1,0:T(8,128)(2,1)S(1)}, bf16[192,512]{1,0:T(8,128)(2,1)S(1)}, u32[]{:S(2)}, u32[]{:S(2)}) %collective-permute-start.8) | collective-permute-done | bytes 196640 | tf_op jit(solution)/shard_map/ppermute | solution.py:640
  113.1 1.0 fusion
  114.7 0.8 copy_select_fusion
  115.5 2.3 %all-to-all-done.1.arrived_ref = bf16[8,528,128]{2,1,0:T(8,128)(2,1)S(1)} async-done(((bf16[8,528,128]{2,1,0:T(8,128)(2,1)}), bf16[8,528,128]{2,1,0:T(8,128)(2,1)S(1)}, u32[]{:S(2)}, u32[]{:S(2)}) %all-to-all-start.1) | async-done | bytes 1081376 | tf_op jit(solution)/shard_map/all_to_all | solution.py:633
  118.8 2.6 %shard_map.125 = (bf16[128,128,128]{2,1,0:T(8,128)(2,1)}, bf16[128,128,128]{2,1,0:T(8,128)(2,1)}) custom-call(s32[16]{0:T(128)} %reshape.74.src_ref, s32[16]{0:T(128)} %reshape.85.target_ref, bf16[8,528,128]{2,1,0:T(8,128)(2,1)} %copy-done.3, bf16[128,128,128]{2,1,0:T(8,128)(2,1)} %get-tuple-element.19.k_ref, ...), custom_call_target="tpu_custom_call", output_to_operand_aliasing={{0}: (3, {}), {1}: (4, {})} | custom-call | bytes 2097152 | tf_op jit(solution)/shard_map/pallas_call | solution.py:451
  (49 shorter events, 5.9 us)
Async XLA Ops:
  0.6 27.2 %copy-start.11 = (s32[1,8,2]{1,2,0:T(2,128)S(1)}, s32[1,8,2]{1,2,0:T(2,128)}, u32[]{:S(2)}) copy-start(s32[1,8,2]{1,2,0:T(2,128)} %param.14) | copy-start | bytes 196
  0.6 27.9 %copy-start.12 = (s32[1,8,2]{1,2,0:T(2,128)S(1)}, s32[1,8,2]{1,2,0:T(2,128)}, u32[]{:S(2)}) copy-start(s32[1,8,2]{1,2,0:T(2,128)} %param.15) | copy-start | bytes 196
  21.8 44.5 %all-to-all-start = ((bf16[8,800,128]{2,1,0:T(8,128)(2,1)}), bf16[8,800,128]{2,1,0:T(8,128)(2,1)S(1)}, u32[]{:S(2)}, u32[]{:S(2)}) async-start(bf16[8,800,128]{2,1,0:T(8,128)(2,1)} %get-tuple-element.15), calls=%async_computation | async-start | bytes 3276800 | tf_op jit(solution)/shard_map/all_to_all | solution.py:627
  29.3 4.5 %copy-start.1 = (bf16[16,12,2,128]{3,2,1,0:T(2,128)(2,1)S(1)}, bf16[16,12,2,128]{3,2,1,0:T(2,128)(2,1)}, u32[]{:S(2)}) copy-start(bf16[16,12,2,128]{3,2,1,0:T(2,128)(2,1)} %param.17) | copy-start | bytes 294916
  29.3 4.5 %copy-start.2 = (bf16[16,12,2,128]{3,2,1,0:T(2,128)(2,1)S(1)}, bf16[16,12,2,128]{3,2,1,0:T(2,128)(2,1)}, u32[]{:S(2)}) copy-start(bf16[16,12,2,128]{3,2,1,0:T(2,128)(2,1)} %param.18) | copy-start | bytes 294916
  67.5 25.1 %copy-start = (bf16[24,4096]{1,0:T(8,128)(2,1)}, bf16[24,4096]{1,0:T(8,128)(2,1)S(1)}, u32[]{:S(2)}) copy-start(bf16[24,4096]{1,0:T(8,128)(2,1)S(1)} %shard_map.124.refs_0_) | copy-start | bytes 589828
  67.5 9.0 %collective-permute-start = (bf16[24,4096]{1,0:T(8,128)(2,1)S(1)}, bf16[24,4096]{1,0:T(8,128)(2,1)S(1)}, u32[]{:S(2)}, u32[]{:S(2)}) collective-permute-start(bf16[24,4096]{1,0:T(8,128)(2,1)S(1)} %shard_map.124.refs_0_), channel_id=1, source_target_pairs={{0,8},{4,12},{8,0},{12,4},{16,24},{20,28},{24,16},{28,20},{1,9},{5... | collective-permute-start | bytes 589832 | tf_op jit(solution)/shard_map/ppermute | solution.py:602
  67.6 17.2 %collective-permute-start.1 = (bf16[24,4096]{1,0:T(8,128)(2,1)S(1)}, bf16[24,4096]{1,0:T(8,128)(2,1)S(1)}, u32[]{:S(2)}, u32[]{:S(2)}) collective-permute-start(bf16[24,4096]{1,0:T(8,128)(2,1)S(1)} %shard_map.124.refs_0_), channel_id=1, source_target_pairs={{0,16},{4,20},{8,24},{12,28},{16,0},{20,4},{24,8},{28,12},{1,17},{... | collective-permute-start | bytes 589832 | tf_op jit(solution)/shard_map/ppermute | solution.py:602
  70.3 16.0 %collective-permute-start.2 = (bf16[24,4096]{1,0:T(8,128)(2,1)S(1)}, bf16[24,4096]{1,0:T(8,128)(2,1)S(1)}, u32[]{:S(2)}, u32[]{:S(2)}) collective-permute-start(bf16[24,4096]{1,0:T(8,128)(2,1)S(1)} %shard_map.124.refs_0_), channel_id=1, source_target_pairs={{0,24},{4,28},{8,16},{12,20},{16,8},{20,12},{24,0},{28,4},{1,25},{... | collective-permute-start | bytes 589832 | tf_op jit(solution)/shard_map/ppermute | solution.py:602
  72.0 20.1 %collective-permute-start.3 = (bf16[24,4096]{1,0:T(8,128)(2,1)S(1)}, bf16[24,4096]{1,0:T(8,128)(2,1)S(1)}, u32[]{:S(2)}, u32[]{:S(2)}) collective-permute-start(bf16[24,4096]{1,0:T(8,128)(2,1)S(1)} %shard_map.124.refs_0_), channel_id=1, source_target_pairs={{0,4},{4,0},{8,12},{12,8},{16,20},{20,16},{24,28},{28,24},{1,5},{5... | collective-permute-start | bytes 589832 | tf_op jit(solution)/shard_map/ppermute | solution.py:604
  76.6 16.0 %copy-start.4 = (bf16[24,4096]{1,0:T(8,128)(2,1)}, bf16[24,4096]{1,0:T(8,128)(2,1)S(1)}, u32[]{:S(2)}) copy-start(bf16[24,4096]{1,0:T(8,128)(2,1)S(1)} %collective-permute-done.refs_2_) | copy-start | bytes 589828
  76.6 15.5 %collective-permute-start.4 = (bf16[24,4096]{1,0:T(8,128)(2,1)S(1)}, bf16[24,4096]{1,0:T(8,128)(2,1)S(1)}, u32[]{:S(2)}, u32[]{:S(2)}) collective-permute-start(bf16[24,4096]{1,0:T(8,128)(2,1)S(1)} %collective-permute-done.refs_2_), channel_id=1, source_target_pairs={{0,4},{4,0},{8,12},{12,8},{16,20},{20,16},{24,28},{28,24},{1,5},{5... | collective-permute-start | bytes 589832 | tf_op jit(solution)/shard_map/ppermute | solution.py:604
  84.8 7.8 %copy-start.5 = (bf16[24,4096]{1,0:T(8,128)(2,1)}, bf16[24,4096]{1,0:T(8,128)(2,1)S(1)}, u32[]{:S(2)}) copy-start(bf16[24,4096]{1,0:T(8,128)(2,1)S(1)} %collective-permute-done.1.refs_4_) | copy-start | bytes 589828
  84.8 7.3 %collective-permute-start.5 = (bf16[24,4096]{1,0:T(8,128)(2,1)S(1)}, bf16[24,4096]{1,0:T(8,128)(2,1)S(1)}, u32[]{:S(2)}, u32[]{:S(2)}) collective-permute-start(bf16[24,4096]{1,0:T(8,128)(2,1)S(1)} %collective-permute-done.1.refs_4_), channel_id=1, source_target_pairs={{0,4},{4,0},{8,12},{12,8},{16,20},{20,16},{24,28},{28,24},{1,5},{5... | collective-permute-start | bytes 589832 | tf_op jit(solution)/shard_map/ppermute | solution.py:604
  86.3 6.3 %copy-start.6 = (bf16[24,4096]{1,0:T(8,128)(2,1)}, bf16[24,4096]{1,0:T(8,128)(2,1)S(1)}, u32[]{:S(2)}) copy-start(bf16[24,4096]{1,0:T(8,128)(2,1)S(1)} %collective-permute-done.2.refs_6_) | copy-start | bytes 589828
  86.3 6.3 %collective-permute-start.6 = (bf16[24,4096]{1,0:T(8,128)(2,1)S(1)}, bf16[24,4096]{1,0:T(8,128)(2,1)S(1)}, u32[]{:S(2)}, u32[]{:S(2)}) collective-permute-start(bf16[24,4096]{1,0:T(8,128)(2,1)S(1)} %collective-permute-done.2.refs_6_), channel_id=1, source_target_pairs={{0,4},{4,0},{8,12},{12,8},{16,20},{20,16},{24,28},{28,24},{1,5},{5... | collective-permute-start | bytes 589832 | tf_op jit(solution)/shard_map/ppermute | solution.py:604
  86.8 31.0 %all-to-all-start.1 = ((bf16[8,528,128]{2,1,0:T(8,128)(2,1)}), bf16[8,528,128]{2,1,0:T(8,128)(2,1)S(1)}, u32[]{:S(2)}, u32[]{:S(2)}) async-start(bf16[8,528,128]{2,1,0:T(8,128)(2,1)} %shard_map.121), calls=%async_computation.1 | async-start | bytes 2162688 | tf_op jit(solution)/shard_map/all_to_all | solution.py:633
  92.0 0.7 copy-start.7
  92.1 0.7 copy-start.8
  92.1 0.8 copy-start.9
  92.6 0.7 copy-start.10
  103.3 1.8 %collective-permute-start.7 = (bf16[2,192,512]{2,1,0:T(8,128)(2,1)S(1)}, bf16[2,192,512]{2,1,0:T(8,128)(2,1)S(1)}, u32[]{:S(2)}, u32[]{:S(2)}) collective-permute-start(bf16[2,192,512]{2,1,0:T(8,128)(2,1)S(1)} %pad_maximum_fusion), channel_id=1, source_target_pairs={{0,1},{1,0},{2,3},{3,2},{4,5},{5,4},{6,7},{7,6},{8,9},{9,8},{10,11... | collective-permute-start | bytes 1179656 | tf_op jit(solution)/shard_map/ppermute | solution.py:637
  106.0 7.0 %collective-permute-start.8 = (bf16[192,512]{1,0:T(8,128)(2,1)S(1)}, bf16[192,512]{1,0:T(8,128)(2,1)S(1)}, u32[]{:S(2)}, u32[]{:S(2)}) collective-permute-start(bf16[192,512]{1,0:T(8,128)(2,1)S(1)} %fusion.1), channel_id=1, source_target_pairs={{0,2},{1,3},{2,0},{3,1},{4,6},{5,7},{6,4},{7,5},{8,10},{9,11},{10,... | collective-permute-start | bytes 589832 | tf_op jit(solution)/shard_map/ppermute | solution.py:640
  117.8 1.0 copy-start.3
